TPU v7x, 512 devices: a whole 4x8x8 slice. The times are simulated.
512 devices in a mesh: row: 16 (over y, x_hi), col: 32 (over x_lo, z, core).
Axes of the slice: x: 4 (x_hi: 2, x_lo: 2; x = x_hi * 2 + x_lo), y: 8, z: 8, core: 2. Of those that a mesh axis runs over, the one named last changes fastest.
Arguments:
- height: float32 [2048, 4096], P('row', 'col'), may hold values from -6 to 6
- density: float32 [2048, 4096], P('row', 'col'), may hold values from 0.2 to 1
- target: float32 [2048, 4096], P('row', 'col'), may hold values from -6 to 6
- region_of_block: int32 [16, 32], P('row', 'col'), may hold values from 0 to 127
- class_of_block: int32 [16, 32], P('row', 'col'), may hold values from 0 to 7
- fill_level: float32 [128], replicated, may hold values from 0 to 0.5
- rates: float32 [8], replicated, may hold values from 0.1 to 0.6
- col_taps: float32 [8, 33], replicated, may hold values from -1 to 1
- row_taps: float32 [8, 33], replicated, may hold values from -1 to 1
- gains: float32 [8], replicated, may hold values from 0.2 to 0.6
Outputs:
- new_height: float32 [2048, 4096], P('row', 'col')
- gain_grad: float32 [8], replicated
- fill_grad: float32 [128], replicated
All inputs are finite; a program needn't handle non-finite values.
Results may differ from a plain program's by a relative error of at most 0.00035.
The roundings to bfloat16 on the way count: a program that leaves them out, or rounds other values in their place, can miss the bound.
Values may be sent and summed in bfloat16 or wider, within the bound.
No kernel may reach another device: no remote copies, remote signals or barrier semaphores. Data moves between devices by JAX's collectives and lax.ppermute only.
A program may use at most 128 MiB of HBM per device.

v0:
```python
import jax
import jax.numpy as jnp
from jax import lax
from jax.sharding import PartitionSpec as P

CHANNELS = 8
TAPS = 33
BLOCK = 128


def kernel_table(tap_weights, length):
    table = []
    for channel in range(CHANNELS):
        grouped = {}
        ordered = []
        for position in range(TAPS):
            offset = (position - TAPS // 2) * 2**channel % length
            if offset not in grouped:
                grouped[offset] = []
                ordered.append(offset)
            grouped[offset].append(position)
        entries = []
        for offset in ordered:
            summed = jnp.zeros((), jnp.float32)
            for position in grouped[offset]:
                summed = summed + tap_weights[channel, position]
            rounded = lax.optimization_barrier(summed.astype(jnp.bfloat16)).astype(jnp.float32)
            entries.append((offset, rounded))
        table.append(entries)
    return table


def shift_sum(band, entries, first, local_len, axis, direction):
    total = band.shape[axis]
    doubled = jnp.concatenate([band, band], axis=axis)
    summed = None
    for offset, weight in entries:
        start = jnp.mod(first + direction * offset, total)
        window = lax.dynamic_slice_in_dim(doubled, start, local_len, axis)
        term = weight * window.astype(jnp.float32)
        summed = term if summed is None else summed + term
    return summed


def spread_add(placed_terms, template_shape, total, axis):
    local_len = template_shape[axis]
    wide_shape = list(template_shape)
    wide_shape[axis] = total + local_len
    running = jnp.zeros(tuple(wide_shape), jnp.float32)
    for start, contribution in placed_terms:
        window = lax.dynamic_slice_in_dim(running, start, local_len, axis)
        running = lax.dynamic_update_slice_in_dim(running, window + contribution, start, axis)
    head = lax.slice_in_dim(running, 0, local_len, axis=axis) + lax.slice_in_dim(
        running, total, total + local_len, axis=axis
    )
    middle = lax.slice_in_dim(running, local_len, total, axis=axis)
    return jnp.concatenate([head, middle], axis=axis)


def shards(
    height,
    density,
    target,
    region_of_block,
    class_of_block,
    fill_level,
    rates,
    col_taps,
    row_taps,
    gains,
):
    rows_here, cols_here = height.shape
    total_rows = rows_here * lax.axis_size("row")
    total_cols = cols_here * lax.axis_size("col")
    row_first = lax.axis_index("row") * rows_here
    col_first = lax.axis_index("col") * cols_here
    block_rows, block_cols = region_of_block.shape
    block_side = rows_here // block_rows
    region_hot = (
        region_of_block[:, :, None] == jnp.arange(fill_level.shape[0], dtype=jnp.int32)
    ).astype(jnp.float32)
    class_hot = (class_of_block[:, :, None] == jnp.arange(rates.shape[0], dtype=jnp.int32)).astype(
        jnp.float32
    )
    fill_block = jnp.sum(region_hot * fill_level, axis=2)
    rate_block = jnp.sum(class_hot * rates, axis=2)

    def to_cells(values):
        spread_out = jnp.broadcast_to(
            values[:, None, :, None], (block_rows, block_side, block_cols, block_side)
        )
        return spread_out.reshape(rows_here, cols_here)

    effective = density + to_cells(fill_block)
    rate_cells = to_cells(rate_block)
    source = (effective * height).astype(jnp.bfloat16)
    col_table = kernel_table(col_taps, total_cols)
    row_table = kernel_table(row_taps, total_rows)
    source_band = lax.all_gather(source, "col", axis=1, tiled=True)
    smoothed = jnp.stack(
        [
            shift_sum(source_band, col_table[channel], col_first, cols_here, 1, -1)
            for channel in range(CHANNELS)
        ]
    ).astype(jnp.bfloat16)
    channel_band = lax.all_gather(smoothed, "row", axis=1, tiled=True)
    pressure_arg = jnp.zeros((rows_here, cols_here), jnp.float32)
    for channel in range(CHANNELS):
        pressure_arg = pressure_arg + gains[channel] * shift_sum(
            channel_band[channel], row_table[channel], row_first, rows_here, 0, -1
        )
    shifted = 1.0 + pressure_arg
    new_height = height - rate_cells * jax.nn.softplus(shifted)
    pressure_adjoint = (
        -(new_height - target) * rate_cells * jax.nn.sigmoid(shifted) / BLOCK
    ).astype(jnp.bfloat16)
    adjoint_band = lax.all_gather(pressure_adjoint, "row", axis=0, tiled=True)
    channel_adjoint = jnp.stack(
        [
            shift_sum(adjoint_band, row_table[channel], row_first, rows_here, 0, 1)
            for channel in range(CHANNELS)
        ]
    )
    gain_local = jnp.sum(channel_adjoint * smoothed.astype(jnp.float32), axis=(1, 2))
    gain_grad = lax.psum(gain_local, ("row", "col"))
    weighted = (gains[:, None, None] * channel_adjoint).astype(jnp.bfloat16)
    placed_columns = []
    for channel in range(CHANNELS):
        channel_values = weighted[channel].astype(jnp.float32)
        for offset, weight in col_table[channel]:
            start = jnp.mod(col_first - offset, total_cols)
            placed_columns.append((start, weight * channel_values))
    column_terms = spread_add(placed_columns, (rows_here, cols_here), total_cols, 1)
    source_adjoint = lax.psum_scatter(
        column_terms.astype(jnp.bfloat16), "col", scatter_dimension=1, tiled=True
    ).astype(jnp.float32)
    block_sums = jnp.sum(
        (source_adjoint * height).reshape(block_rows, block_side, block_cols, block_side),
        axis=(1, 3),
    )
    fill_local = jnp.sum(region_hot * block_sums[:, :, None], axis=(0, 1))
    fill_grad = lax.psum(fill_local, ("row", "col"))
    return (new_height, gain_grad, fill_grad)


def solution(mesh):
    in_specs = (
        P("row", "col"),
        P("row", "col"),
        P("row", "col"),
        P("row", "col"),
        P("row", "col"),
        P(),
        P(),
        P(),
        P(),
        P(),
    )
    out_specs = (P("row", "col"), P(), P())
    return jax.shard_map(shards, mesh=mesh, in_specs=in_specs, out_specs=out_specs, check_vma=False)
```

profile of v0, /device:TPU:1, one launch (start us, length us, event | category | flops | bytes accessed | tf_op | source)
XLA Modules:
  0.0 1034.6 jit_solution(17635049522354549897)
XLA Ops:
  7.9 1.3 fusion.1270
  9.1 2.1 multiply_convert_fusion.2
  191.6 1.4 constant_dynamic-update-slice_fusion.1
  194.0 1.0 constant_dynamic-update-slice_fusion.8
  195.0 1.0 constant_dynamic-update-slice_fusion.7
  196.0 1.0 constant_dynamic-update-slice_fusion.6
  197.0 1.0 constant_dynamic-update-slice_fusion.5
  198.0 1.0 constant_dynamic-update-slice_fusion.4
  198.9 1.3 constant_dynamic-update-slice_fusion.3
  200.3 1.0 constant_dynamic-update-slice_fusion.2
  387.4 2.4 slice_bitcast_fusion.4
  389.8 0.9 fusion.1041
  390.7 0.9 fusion.1026
  392.1 0.9 fusion.1042
  393.0 1.0 fusion.1073
  394.0 0.9 fusion.1074
  394.9 0.9 fusion.1106
  395.8 0.9 fusion.1053
  396.6 0.9 fusion.1085
  397.9 0.9 fusion.1124
  398.8 0.9 fusion.1091
  399.7 0.9 fusion.1059
  400.5 0.9 fusion.1103
  401.4 0.9 fusion.1025
  402.4 0.9 fusion.1097
  403.3 0.9 fusion.1163
  404.1 0.9 fusion.1130
  405.0 1.3 fusion.1118
  406.3 0.9 fusion.1065
  407.2 0.9 fusion.1107
  411.0 89.8 %multiply_add_fusion.1 = f32[128,128]{1,0:T(8,128)S(1)} fusion(s32[]{:T(128)S(6)} %select_n.5624, bf16[2048,128]{1,0:T(8,128)(2,1)S(1)} %get-tuple-element.12, s32[]{:T(128)S(6)} %select_n.5594, s32[]{:T(128)S(6)} %select_n.5596, s32[]{:T(128)S(6)} %select_n.5598, s32[]{:T(128)S(6)} %select_n.5600, s32[]{:T(128)S(6)} %select_n.5602, s32[]{:T(128)S(6)} %select_n.5604, ...), kind=kLoop, calls=%fused_computation.2697 | loop fusion | flops 9764864 | bytes 2687446 | tf_op jit(solution)/shard_map/add | solution.py:109
  500.8 16.8 %multiply_convert_fusion.1 = (bf16[128,128]{1,0:T(8,128)(2,1)S(1)}, f32[128,128]{1,0:T(8,128)}) fusion(f32[128,128]{1,0:T(8,128)S(1)} %copy-done.5, f32[]{:T(128)} %fusion.1271, f32[128,128]{1,0:T(8,128)S(1)} %copy-done.3, bf16[128,128]{1,0:T(8,128)(2,1)S(1)} %get-tuple-element.171, f32[]{:T(128)S(6)} %convert_element_type.6866, ...), kind=kLoop, calls=%fused_computation.2693 | loop fusion | flops 8699904 | bytes 4915900 | tf_op jit(solution)/shard_map/convert_element_type | solution.py:116
  517.6 38.2 %all_gather.11 = bf16[2048,128]{1,0:T(8,128)(2,1)S(1)} all-gather(bf16[128,128]{1,0:T(8,128)(2,1)S(1)} %get-tuple-element.5), channel_id=1, replica_groups=mesh['row'=16,'col'=32] {'row'}, dimensions={0}, use_global_device_ids=true | all-gather | bytes 557056 | tf_op jit(solution)/shard_map/all_gather | solution.py:117
  556.7 0.9 bitcast_dynamic-update-slice_fusion.5
  557.6 1.0 bitcast_dynamic-update-slice_fusion.4
  558.6 0.9 bitcast_dynamic-update-slice_fusion.3
  559.5 0.9 bitcast_dynamic-update-slice_fusion.2
  560.4 0.9 bitcast_dynamic-update-slice_fusion.1
  562.9 1.0 dynamic_update_slice.789
  594.1 1.1 dynamic_update_slice.822
  625.4 1.2 dynamic_update_slice.855
  687.7 0.9 dynamic_update_slice.921
  718.3 1.1 dynamic_update_slice.954
  776.6 0.9 dynamic_update_slice.1020
  801.4 1.3 copy.13
  802.7 123.6 %reduce-scatter.4.cloned.1.call-done = bf16[128,128]{1,0:T(8,128)(2,1)} async-done(((bf16[4096,128]{1,0:T(8,128)(2,1)}), bf16[128,128]{1,0:T(8,128)(2,1)}) %reduce-scatter.4.cloned.1.call-update) | async-done | bytes 32784
  926.3 0.9 copy.14
  928.5 99.2 %all-reduce = (f32[8]{0:T(128)}, f32[128]{0:T(128)}) all-reduce(f32[8]{0:T(128)S(1)} %get-tuple-element.16, f32[128]{0:T(128)S(1)} %compare_select_fusion.2), channel_id=1, replica_groups=mesh['row'=16,'col'=32] {'row','col'}, use_global_device_ids=true, to_apply=%region_3.4 | all-reduce | flops 136 | bytes 1088 | tf_op jit(solution)/shard_map/psum | solution.py:125
  (602 shorter events, 261.5 us)
Async XLA Ops:
  7.2 6.6 copy-start.7
  7.2 184.4 %all-gather.3.cloned.1.call-start = ((), (), s32[]{:S(2)}) async-start(), calls=%async_computation.1 | async-start | bytes 1081344 | tf_op jit(solution)/shard_map/all_gather | solution.py:99
  11.3 376.1 %all-gather.5.cloned.1.call-start = ((), (), s32[]{:S(2)}) async-start(), calls=%async_computation.2 | async-start | bytes 4456448 | tf_op jit(solution)/shard_map/all_gather | solution.py:106
  191.6 1.5 copy-start
  201.2 0.7 copy-start.1
  202.0 724.3 %reduce-scatter.4.cloned.1.call-start = ((), (), s32[]{:S(2)}) async-start(), calls=%async_computation.3 | async-start | bytes 1081344
  203.8 1.9 copy-start.4
  205.1 181.0 %copy-start.8 = (f32[8]{0:T(128)S(1)}, f32[8]{0:T(128)}, u32[]{:S(2)}) copy-start(f32[8]{0:T(128)} %param.16) | copy-start | bytes 100
  205.1 181.6 %copy-start.6 = (f32[8]{0:T(128)S(1)}, f32[8]{0:T(128)}, u32[]{:S(2)}) copy-start(f32[8]{0:T(128)} %param.19) | copy-start | bytes 100
  410.2 90.5 %copy-start.3 = (f32[128,128]{1,0:T(8,128)S(1)}, f32[128,128]{1,0:T(8,128)}, u32[]{:S(2)}) copy-start(f32[128,128]{1,0:T(8,128)} %param.10) | copy-start | bytes 196612
  410.2 90.5 %copy-start.5 = (f32[128,128]{1,0:T(8,128)S(1)}, f32[128,128]{1,0:T(8,128)}, u32[]{:S(2)}) copy-start(f32[128,128]{1,0:T(8,128)} %param.12) | copy-start | bytes 196612
  559.5 3.0 copy-start.2
Sparse Core Ops, SparseCore 0:
  11.4 71.6 all-gather.2
  202.1 107.3 all-gather.4
  802.8 123.4 reduce-scatter.3
where the time goes:
time: 1050 us; the launch traced here: 1030 us
  between operations  361 us (34%)
  local copies, waits for them, and re-layouts  242 us (23%)
  other arithmetic  170 us (16%)
  blocking collectives  137 us (13%)
  waiting for transfers between devices  124 us (12%)
    dynamic_update_slice x263, local copies, waits for them, and re-layouts, spread_add(): lax.dynamic_update_slice_in_dim(running, window + contribution, start, axis)  210 us
    unnamed x4, waiting for transfers between devices  124 us
    psum x1, blocking collectives, shards(): gain_grad = lax.psum(gain_local, ('row', 'col'))  99.2 us
    add x1, other arithmetic, shards(): pressure_arg + gains[channel] * shift_sum(channel_band[channel], row_tabl...  89.8 us
    all_gather x1, blocking collectives, shards(): adjoint_band = lax.all_gather(pressure_adjoint, 'row', axis=0, tiled=True)  38.2 us
    add x262, other arithmetic, spread_add(): window + contribution  24.3 us
    slice x31, local copies, waits for them, and re-layouts, kernel_table(): summed = summed + tap_weights[channel, position]  22.2 us
  transfers between devices with their start and end apart: 3, of which 1 were waited for; matrix products, arithmetic and copies ran while one was open for 2% of the time, Pallas kernels for 0%

commit v1 on v0

v1 whole, which is shorter than its diff:
```python
import jax
import jax.numpy as jnp
from jax import lax
from jax.experimental import pallas as pl
from jax.experimental.pallas import tpu as pltpu
from jax.sharding import PartitionSpec as P

CHANNELS = 8
TAPS = 33
HALF = TAPS // 2
SIDE = 128
ROWS = 16
COLS = 32
PEERS = COLS // 2
SUB = SIDE // ROWS
MIXED = CHANNELS - 1
F32 = jnp.float32
BF16 = jnp.bfloat16
VMEM = pl.BlockSpec(memory_space=pltpu.VMEM)
SMEM = pl.BlockSpec(memory_space=pltpu.SMEM)
ANY = pl.BlockSpec(memory_space=pl.ANY)
PARAMS = pltpu.CompilerParams(vmem_limit_bytes=24 * 1024 * 1024)


def reach(channel):
    return max(1, 2**channel * HALF // SIDE)


def blocks(channel):
    return 2 * reach(channel) + 1


def split(values):
    high = values.astype(BF16)
    low = (values - high.astype(F32)).astype(BF16)
    return high, low


def pair_rows(first, second):
    return jnp.concatenate(
        [first.reshape(ROWS, SUB, SIDE), second.reshape(ROWS, SUB, SIDE)], axis=1
    )


def unpair_rows(pairs):
    values = pairs.astype(F32)
    return (
        values[:, :SUB, :].reshape(SIDE, SIDE),
        values[:, SUB:, :].reshape(SIDE, SIDE),
    )


def source_kernel(region_ref, fill_ref, height_ref, density_ref, out_ref):
    fill = fill_ref[region_ref[0, 0]]
    source = (density_ref[...] + fill) * height_ref[...]
    turned = source.T.astype(BF16)
    for peer in range(PEERS):
        out_ref[peer] = turned


def toeplitz(taps_ref, channel, direction, merged):
    width = (blocks(channel) + 1) * SIDE
    lane = lax.broadcasted_iota(jnp.int32, (1, SIDE), 1)
    parts = [jnp.zeros((1, SIDE), F32) for _ in range(width // SIDE)]
    for position in range(TAPS):
        value = taps_ref[channel, position]
        if merged and position == 0:
            continue
        if merged and position == TAPS - 1:
            value = value + taps_ref[channel, 0]
        place = reach(channel) * SIDE + direction * (position - HALF) * 2**channel
        part, inside = divmod(place, SIDE)
        parts[part] = jnp.where(lane == inside, value, parts[part])
    base = jnp.concatenate(parts, axis=1).astype(BF16).astype(F32)
    spread = jnp.broadcast_to(base, (SIDE, width))
    rolled = pltpu.roll(spread, 0, 1, stride=1, stride_axis=0)
    return rolled[:, : blocks(channel) * SIDE].astype(BF16)


def tables_kernel(
    col_ref, row_ref, class_ref, height_ref, target_ref, gathered_ref, *out_refs
):
    col_out, row_out = out_refs[:MIXED], out_refs[MIXED : 2 * MIXED]
    col_last, row_last, extra_ref = out_refs[2 * MIXED :]
    for channel in range(MIXED):
        col_out[channel][...] = toeplitz(col_ref, channel, -1, False)
        row_out[channel][...] = toeplitz(row_ref, channel, 1, channel == 6)
    for step in range(COLS):
        value = col_ref[MIXED, TAPS - 1 - step]
        if step == 0:
            value = value + col_ref[MIXED, 0]
        col_last[step] = jnp.full((SUB, SIDE), value, F32).astype(BF16).astype(F32)
    for step in range(ROWS):
        value = row_ref[MIXED, step] + row_ref[MIXED, step + ROWS]
        if step == 0:
            value = value + row_ref[MIXED, TAPS - 1]
        row_last[step] = jnp.full((SUB, SIDE), value, F32).astype(BF16).astype(F32)
    away = (height_ref[...] - target_ref[...]).T
    high, low = split(away)
    extra_ref[:, :16, :] = pair_rows(high.astype(F32), low.astype(F32)).astype(BF16)
    kind = class_ref[0, 0].astype(F32)
    extra_ref[:, 16:, :] = jnp.full((ROWS, 16, SIDE), kind, F32).astype(BF16)


def smooth_kernel(col_index_ref, own_ref, other_ref, last_ref, extra_ref, *refs):
    tables, out_ref, window_ref = refs[:MIXED], refs[MIXED], refs[MIXED + 1]
    here = col_index_ref[0]
    last = jnp.zeros((SIDE, SIDE), F32)
    for step in range(COLS):
        block = lax.rem(here + (COLS - HALF + step), COLS) // 2
        values = (own_ref if step % 2 == 0 else other_ref)[block]
        window_ref[step * SIDE : (step + 1) * SIDE, :] = values
        scaled = values.astype(F32).reshape(ROWS, SUB, SIDE) * last_ref[step]
        last = last + scaled.reshape(SIDE, SIDE)
    smoothed = []
    for channel in range(MIXED):
        first = (HALF - reach(channel)) * SIDE
        smoothed.append(
            jnp.dot(
                tables[channel][...],
                window_ref[first : first + blocks(channel) * SIDE, :],
                preferred_element_type=F32,
            )
        )
    smoothed.append(last)
    for pair in range(CHANNELS // 2):
        out_ref[:, 16 * pair : 16 * pair + 16, :] = pair_rows(
            smoothed[2 * pair], smoothed[2 * pair + 1]
        ).astype(BF16)
    out_ref[:, 64:, :] = extra_ref[...]


def rolled_rows(values, block_shift):
    shift = block_shift * SUB % SIDE
    if shift == 0:
        return values
    return jnp.concatenate([values[SIDE - shift :], values[: SIDE - shift]], axis=0)


def pressure_kernel(gains_ref, rates_ref, long_ref, last_ref, *refs):
    tables, out_ref, gain_ref = refs[:MIXED], refs[MIXED], refs[MIXED + 1]
    smoothed = []
    for pair in range(CHANNELS // 2):
        smoothed.extend(unpair_rows(long_ref[:, 16 * pair : 16 * pair + 16, :]))
    high, low = unpair_rows(long_ref[:, 64:80, :])
    away = high + low
    kind, _ = unpair_rows(long_ref[:, 80:96, :])
    rate = jnp.zeros((SIDE, SIDE), F32)
    for number in range(rates_ref.shape[0]):
        rate = jnp.where(kind == float(number), rates_ref[number], rate)

    pressure = jnp.zeros((SIDE, SIDE), F32)
    for channel in range(MIXED):
        spread = jnp.dot(
            smoothed[channel].astype(BF16), tables[channel][...], preferred_element_type=F32
        )
        total = None
        for block in range(blocks(channel)):
            term = rolled_rows(
                spread[:, block * SIDE : (block + 1) * SIDE], block - reach(channel)
            )
            total = term if total is None else total + term
        pressure = pressure + gains_ref[channel] * total
    total = jnp.zeros((SIDE, SIDE), F32)
    for step in range(ROWS):
        scaled = smoothed[MIXED].reshape(ROWS, SUB, SIDE) * last_ref[step]
        total = total + rolled_rows(scaled.reshape(SIDE, SIDE), step)
    pressure = pressure + gains_ref[MIXED] * total

    shifted = 1.0 + pressure
    decay = jnp.exp(-jnp.abs(shifted))
    removed = rate * (jnp.maximum(shifted, 0.0) + jnp.log1p(decay))
    slope = jnp.where(shifted >= 0, 1.0, decay) / (1.0 + decay)
    adjoint = (-(away - removed) * rate * slope / SIDE).astype(BF16)

    weighted = []
    gain_rows = []
    for channel in range(CHANNELS):
        total = jnp.zeros((SIDE, SIDE), F32)
        if channel < MIXED:
            for block in range(blocks(channel)):
                term = lax.dot_general(
                    adjoint,
                    tables[channel][:, block * SIDE : (block + 1) * SIDE],
                    (((1,), (1,)), ((), ())),
                    preferred_element_type=F32,
                )
                total = total + rolled_rows(term, reach(channel) - block)
        else:
            wide = adjoint.astype(F32).reshape(ROWS, SUB, SIDE)
            for step in range(ROWS):
                scaled = wide * last_ref[step]
                total = total + rolled_rows(scaled.reshape(SIDE, SIDE), -step)
        gain_rows.append(jnp.sum(total * smoothed[channel], axis=0, keepdims=True))
        weighted.append(gains_ref[channel] * total)
    for pair in range(CHANNELS // 2):
        out_ref[:, 16 * pair : 16 * pair + 16, :] = pair_rows(
            weighted[2 * pair], weighted[2 * pair + 1]
        ).astype(BF16)
    high, low = split(removed)
    out_ref[:, 64:, :] = pair_rows(high.astype(F32), low.astype(F32)).astype(BF16)
    gain_ref[...] = jnp.concatenate(gain_rows, axis=0)


def gradient_kernel(
    col_index_ref, back_ref, band_ref, last_ref, gain_ref, height_ref, *refs
):
    tables, new_ref, sums_ref = refs[:MIXED], refs[MIXED], refs[MIXED + 1]
    here = col_index_ref[0]
    weighted = []
    for pair in range(CHANNELS // 2):
        weighted.extend(unpair_rows(back_ref[:, 16 * pair : 16 * pair + 16, :]))
    high, low = unpair_rows(back_ref[:, 64:80, :])
    new_ref[...] = height_ref[...] - (high + low).T
    turned = weighted[MIXED].T
    doubled = []
    for channel in range(MIXED):
        narrow = weighted[channel].astype(BF16)
        doubled.append(jnp.concatenate([narrow, narrow], axis=1))
    lane = lax.broadcasted_iota(jnp.int32, (SUB, SIDE), 1)
    fill = jnp.zeros((SUB, SIDE), F32)
    for step in range(COLS):
        block = lax.rem(here + (COLS - HALF + step), COLS)
        values = band_ref[block, :SIDE, :]
        region = band_ref[block, SIDE:, :]
        product = jnp.sum((turned * values).reshape(ROWS, SUB, SIDE), axis=0)
        terms = product * last_ref[step]
        ahead = step - HALF
        channels = [c for c in range(MIXED) if abs(ahead) <= reach(c)]
        if channels:
            both = jnp.concatenate(split(values), axis=0)
            for channel in channels:
                place = (ahead + reach(channel)) * SIDE
                cross = jnp.dot(doubled[channel], both, preferred_element_type=F32)
                taps = tables[channel][:, place : place + SIDE].astype(F32)
                terms = terms + jnp.sum((cross * taps).reshape(ROWS, SUB, SIDE), axis=0)
        total = jnp.sum(terms, axis=1, keepdims=True)
        fill = fill + jnp.where(region == lane.astype(F32), total, 0.0)
    gain = jnp.sum(gain_ref[...], axis=1, keepdims=True)
    row = lax.broadcasted_iota(jnp.int32, (SUB, SIDE), 0)
    gain = jnp.where(row == lane, gain, 0.0)
    fill_row = jnp.sum(fill, axis=0, keepdims=True)
    gain_row = jnp.sum(gain, axis=0, keepdims=True)
    both = jnp.concatenate([fill_row, gain_row], axis=0)
    for peer in range(COLS):
        sums_ref[peer] = both


def shape(*dims, dtype=F32):
    return jax.ShapeDtypeStruct(dims, dtype)


def shards(
    height,
    density,
    target,
    region_of_block,
    class_of_block,
    fill_level,
    rates,
    col_taps,
    row_taps,
    gains,
):
    col_index = lax.axis_index("col").astype(jnp.int32).reshape(1)
    marks = jnp.broadcast_to(region_of_block.astype(F32), (SUB, SIDE))
    marked = jnp.concatenate([height, marks], axis=0)
    band = lax.all_gather(marked, "col", axis=0, tiled=False)

    copies = pl.pallas_call(
        source_kernel,
        out_shape=shape(PEERS, SIDE, SIDE, dtype=BF16),
        in_specs=[SMEM, SMEM, VMEM, VMEM],
        out_specs=VMEM,
        compiler_params=PARAMS,
        name="source",
    )(region_of_block, fill_level, height, density)
    groups = [[2 * block + core for block in range(PEERS)] for core in range(2)]
    own = lax.all_to_all(copies, "col", 0, 0, axis_index_groups=groups, tiled=True)
    other = lax.ppermute(own, "col", [(block, block ^ 1) for block in range(COLS)])

    table_shapes = [shape(SIDE, blocks(c) * SIDE, dtype=BF16) for c in range(MIXED)]
    made = pl.pallas_call(
        tables_kernel,
        out_shape=table_shapes
        + table_shapes
        + [shape(COLS, SUB, SIDE), shape(ROWS, SUB, SIDE), shape(ROWS, 32, SIDE, dtype=BF16)],
        in_specs=[SMEM, SMEM, SMEM, VMEM, VMEM, ANY],
        out_specs=[VMEM] * (2 * MIXED + 3),
        compiler_params=PARAMS,
        cost_estimate=pl.CostEstimate(flops=4000000, bytes_accessed=4000000, transcendentals=0),
        name="tables",
    )(col_taps, row_taps, class_of_block, height, target, own)
    col_tables, row_tables = made[:MIXED], made[MIXED : 2 * MIXED]
    col_last, row_last, extra = made[2 * MIXED :]

    smoothed = pl.pallas_call(
        smooth_kernel,
        out_shape=shape(ROWS, 96, SIDE, dtype=BF16),
        in_specs=[SMEM] + [VMEM] * (4 + MIXED),
        out_specs=VMEM,
        scratch_shapes=[pltpu.VMEM((COLS * SIDE, SIDE), BF16)],
        compiler_params=PARAMS,
        name="smooth",
    )(col_index, own, other, col_last, extra, *col_tables)
    long = lax.all_to_all(smoothed, "row", 0, 0, tiled=True)

    back, gain_part = pl.pallas_call(
        pressure_kernel,
        out_shape=[shape(ROWS, 80, SIDE, dtype=BF16), shape(CHANNELS, SIDE)],
        in_specs=[SMEM, SMEM] + [VMEM] * (2 + MIXED),
        out_specs=[VMEM, VMEM],
        compiler_params=PARAMS,
        name="pressure",
    )(gains, rates, long, row_last, *row_tables)
    tile = lax.all_to_all(back, "row", 0, 0, tiled=True)

    new_height, sums = pl.pallas_call(
        gradient_kernel,
        out_shape=[shape(SIDE, SIDE), shape(COLS, 2, SIDE)],
        in_specs=[SMEM] + [VMEM] * (5 + MIXED),
        out_specs=[VMEM, VMEM],
        compiler_params=PARAMS,
        name="gradient",
    )(col_index, tile, band, col_last, gain_part, height, *col_tables)
    by_col = lax.all_to_all(sums, "col", 0, 0, tiled=True)
    band_sum = jnp.sum(by_col, axis=0, keepdims=True)
    by_row = lax.all_to_all(
        jnp.broadcast_to(band_sum, (ROWS, 2, SIDE)), "row", 0, 0, tiled=True
    )
    total = jnp.sum(by_row, axis=0)
    return new_height, total[1, :CHANNELS], total[0]


def solution(mesh):
    cells = P("row", "col")
    in_specs = (cells,) * 5 + (P(),) * 5
    out_specs = (cells, P(), P())
    return jax.shard_map(shards, mesh=mesh, in_specs=in_specs, out_specs=out_specs, check_vma=False)
```

time: 1050 us -> 132 us (0.13); the launches traced: 1030 us -> 131 us
  between operations: 361 us -> 15.4 us
  local copies, waits for them, and re-layouts: 242 us -> 9.53 us
  other arithmetic: 170 us -> 0.07 us
  waiting for transfers between devices: 124 us -> 0.02 us
  blocking collectives: 137 us -> 93 us
    dynamic_update_slice x263 -> x0, local copies, waits for them, and re-layouts: 210 us -> none  [spread_add(): lax.dynamic_update_slice_in_dim(running, window + contribution, start, axis)]
    unnamed x4 -> x1, waiting for transfers between devices: 124 us -> 0.02 us
    add x263 -> x0, other arithmetic: 114 us -> none  [the longest x1 89.8 us: shards(): pressure_arg + gains[channel] * shift_sum(channel_band[channel], row_tabl...]
    psum x1 -> x0, blocking collectives: 99.2 us -> none  [shards(): gain_grad = lax.psum(gain_local, ('row', 'col'))]
    all_to_all x0 -> x5, blocking collectives: none -> 93 us  [the longest x1 25.8 us: shards(): lax.all_to_all(copies, 'col', 0, 0, axis_index_groups=groups, tiled=True)]
    all_gather x1 -> x0, blocking collectives: 38.2 us -> none  [shards(): adjoint_band = lax.all_gather(pressure_adjoint, 'row', axis=0, tiled=True)]
    slice x33 -> x0, local copies, waits for them, and re-layouts: 23 us -> none  [the longest x31 22.2 us: kernel_table(): summed = summed + tap_weights[channel, position]]
    convert_element_type x3 -> x0, other arithmetic: 19.1 us -> none  [the longest x1 16.8 us: shards(): pressure_adjoint = (-(new_height - target) * rate_cells * jax.nn.sigmoid(...]
  transfers between devices with their start and end apart: 3 -> 2, of which waited for: 1 -> 0; matrix products, arithmetic and copies ran while one was open for 2% -> 0% of each run, Pallas kernels for 0% -> 4%
where the time goes in v1:
time: 132 us; the launch traced here: 131 us
  blocking collectives  93 us (70%)
  between operations  15.4 us (12%)
  local copies, waits for them, and re-layouts  9.53 us (7%)
  Pallas kernels  6.8 us (5%)
  starting transfers between devices  6.25 us (5%)
    all_to_all x1, blocking collectives, shards(): lax.all_to_all(copies, 'col', 0, 0, axis_index_groups=groups, tiled=True)  25.8 us
    all_to_all x1, blocking collectives, shards(): long = lax.all_to_all(smoothed, 'row', 0, 0, tiled=True)  24.6 us
    all_to_all x1, blocking collectives, shards(): tile = lax.all_to_all(back, 'row', 0, 0, tiled=True)  16.7 us
    all_to_all x1, blocking collectives, shards(): by_col = lax.all_to_all(sums, 'col', 0, 0, tiled=True)  14.2 us
    all_to_all x1, blocking collectives, shards(): lax.all_to_all(jnp.broadcast_to(band_sum, (ROWS, 2, SIDE)), 'row', 0, 0,...  11.7 us
    unnamed x22, local copies, waits for them, and re-layouts  7.02 us
    ppermute x1, starting transfers between devices, shards(): lax.ppermute(own, 'col', [(block, block ^ 1) for block in range(COLS)])  6.21 us
  transfers between devices with their start and end apart: 2, of which 0 were waited for; matrix products, arithmetic and copies ran while one was open for 0% of the time, Pallas kernels for 4%

profile of v1, /device:TPU:1, one launch (start us, length us, event | category | flops | bytes accessed | tf_op | source)
XLA Modules:
  0.0 131.1 jit_solution(10928858702847250046)
XLA Ops:
  7.2 0.0 all-gather.3.cloned.1.call-start
  7.9 1.5 %concatenate.3 = f32[136,128]{1,0:T(8,128)} pad(f32[128,128]{1,0:T(8,128)} %height_ref.5, f32[]{:T(128)} %bitcast.1), padding=0_8x0_0 | pad | bytes 135172 | tf_op jit(solution)/shard_map/concatenate | solution.py:267
  9.3 0.0 all-gather.3.cloned.1.call-update
  9.4 0.0 copy-start.1
  9.4 0.8 copy-done.1
  10.2 0.0 copy-start.4
  10.2 0.8 copy-done.4
  11.0 0.0 copy-start.8
  11.0 0.7 copy-done.8
  11.7 0.7 source.1
  12.4 25.8 %all_to_all.25.gathered_ref.own_ref = bf16[16,128,128]{2,1,0:T(8,128)(2,1)S(1)} all-to-all(bf16[16,128,128]{2,1,0:T(8,128)(2,1)S(1)} %source.1), channel_id=1, replica_groups={{0,2,4,6,8,10,12,14,16,18,20,22,24,26,28,30},{1,3,5,7,9,11,13,15,17,19,..., dimensions={0} | all-to-all | bytes 1048576 | tf_op jit(solution)/shard_map/all_to_all | solution.py:279
  38.2 6.2 %collective-permute-start = (bf16[16,128,128]{2,1,0:T(8,128)(2,1)S(1)}, bf16[16,128,128]{2,1,0:T(8,128)(2,1)S(1)}, u32[]{:S(2)}, u32[]{:S(2)}) collective-permute-start(bf16[16,128,128]{2,1,0:T(8,128)(2,1)S(1)} %all_to_all.25.gathered_ref.own_ref), channel_id=1, source_target_pairs={{0,1},{1,0},{2,3},{3,2},{4,5},{5,4},{6,7},{7,6},{8,9},{9,8},{10,11... | collective-permute-start | bytes 1572872 | tf_op jit(solution)/shard_map/ppermute | solution.py:280
  45.0 0.0 copy-start.2
  45.0 0.8 copy-done.2
  45.9 0.0 copy-start.5
  45.9 0.8 copy-done.5
  46.7 0.0 copy-start.6
  46.7 0.7 copy-done.6
  47.4 0.0 copy-start.7
  47.4 0.7 copy-done.7
  48.1 0.0 copy-start.9
  48.1 0.0 copy-start.10
  48.1 1.5 %tables.1 = (bf16[128,384]{1,0:T(8,128)(2,1)S(1)}, bf16[128,384]{1,0:T(8,128)(2,1)S(1)}, bf16[128,384]{1,0:T(8,128)(2,1)S(1)}, bf16[128,384]{1,0:T(8,128)(2,1)S(...) custom-call(f32[8,33]{1,0:T(8,128)S(1)} %copy-done.6, ...), custom_call_target="tpu_custom_call" | custom-call | flops 4000000 | bytes 4000000 | tf_op jit(solution)/shard_map/tables/pallas_call | solution.py:283
  49.6 0.0 collective-permute-done.other_ref
  49.6 0.7 smooth.1
  50.4 0.0 copy-start.3
  50.4 24.6 %all_to_all.26.long_ref = bf16[16,96,128]{2,1,0:T(8,128)(2,1)S(1)} all-to-all(bf16[16,96,128]{2,1,0:T(8,128)(2,1)S(1)} %smooth.1), channel_id=1, replica_groups=mesh['row'=16,'col'=32] {'row'}, dimensions={0} | all-to-all | bytes 786432 | tf_op jit(solution)/shard_map/all_to_all | solution.py:306
  74.9 0.0 copy-done.9
  75.0 0.0 copy-done.10
  75.0 2.3 %pressure.1 = (bf16[16,80,128]{2,1,0:T(8,128)(2,1)S(1)}, f32[8,128]{1,0:T(8,128)S(1)}) custom-call(f32[8]{0:T(128)S(1)} %copy-done.9, f32[8]{0:T(128)S(1)} %copy-done.10, bf16[16,96,128]{2,1,0:T(8,128)(2,1)S(1)} %all_to_all.26.long_ref, f32[16,8,128]{2,1,0:T(8,128)S(1)} %get-tuple-element.33.last_ref, bf16[128,384]{1,0:T(8,128)(2,1)S(1)} %get-tuple-element.34.refs_0_, ...), custom_call_target="tpu_custom_call" | custom-call | tf_op jit(solution)/shard_map/pressure/pallas_call | solution.py:308
  77.3 16.7 %all_to_all.27.back_ref = bf16[16,80,128]{2,1,0:T(8,128)(2,1)S(1)} all-to-all(bf16[16,80,128]{2,1,0:T(8,128)(2,1)S(1)} %get-tuple-element.41), channel_id=1, replica_groups=mesh['row'=16,'col'=32] {'row'}, dimensions={0} | all-to-all | bytes 655360 | tf_op jit(solution)/shard_map/all_to_all | solution.py:316
  94.0 0.0 all-gather.3.cloned.1.call-done
  94.0 0.0 copy-done.3
  94.0 0.0 copy-start
  94.0 1.6 %copy-done = f32[4352,128]{1,0:T(8,128)S(1)} copy-done((f32[4352,128]{1,0:T(8,128)S(1)}, f32[4352,128]{1,0:T(8,128)}, u32[]{:S(2)}) %copy-start) | copy-done | bytes 2228248
  95.6 1.6 %gradient.1 = (f32[128,128]{1,0:T(8,128)}, f32[32,2,128]{2,1,0:T(2,128)S(1)}) custom-call(s32[1]{0:T(128)} %bitcast.col_index_ref, bf16[16,80,128]{2,1,0:T(8,128)(2,1)S(1)} %all_to_all.27.back_ref, f32[32,136,128]{2,1,0:T(8,128)S(1)} %bitcast.7, f32[32,8,128]{2,1,0:T(8,128)S(1)} %get-tuple-element.24.last_ref, f32[8,128]{1,0:T(8,128)S(1)} %get-tuple-element.42.gain_ref, ...), custom_call_target="tpu_custom_call" | custom-call | tf_op jit(solution)/shard_map/gradient/pallas_call | solution.py:318
  97.2 14.2 %all_to_all.28 = f32[32,2,128]{2,1,0:T(2,128)S(1)} all-to-all(f32[32,2,128]{2,1,0:T(2,128)S(1)} %get-tuple-element.44), channel_id=1, replica_groups=mesh['row'=16,'col'=32] {'col'}, dimensions={0} | all-to-all | bytes 65536 | tf_op jit(solution)/shard_map/all_to_all | solution.py:326
  111.5 11.7 %all_to_all.29 = f32[16,2,128]{2,1,0:T(2,128)S(1)} all-to-all(f32[16,2,128]{2,1,0:T(2,128)S(1)} %broadcast_in_dim.5), channel_id=1, replica_groups=mesh['row'=16,'col'=32] {'row'}, dimensions={0} | all-to-all | bytes 32768 | tf_op jit(solution)/shard_map/all_to_all | solution.py:328
  123.2 0.5 slice_bitcast_fusion
  123.7 0.5 slice_bitcast_fusion.1
  (3 shorter events, 0.1 us)
Async XLA Ops:
  7.2 86.8 %all-gather.3.cloned.1.call-start = ((), (), s32[]{:S(2)}) async-start(), calls=%async_computation.5 | async-start | bytes 2297856 | tf_op jit(solution)/shard_map/all_gather | solution.py:268
  9.4 0.8 copy-start.1
  10.2 0.8 copy-start.4
  11.0 0.7 copy-start.8
  38.2 11.5 %collective-permute-start = (bf16[16,128,128]{2,1,0:T(8,128)(2,1)S(1)}, bf16[16,128,128]{2,1,0:T(8,128)(2,1)S(1)}, u32[]{:S(2)}, u32[]{:S(2)}) collective-permute-start(bf16[16,128,128]{2,1,0:T(8,128)(2,1)S(1)} %all_to_all.25.gathered_ref.own_ref), channel_id=1, source_target_pairs={{0,1},{1,0},{2,3},{3,2},{4,5},{5,4},{6,7},{7,6},{8,9},{9,8},{10,11... | collective-permute-start | bytes 1572872 | tf_op jit(solution)/shard_map/ppermute | solution.py:280
  45.0 0.8 copy-start.2
  45.9 0.8 copy-start.5
  46.7 0.7 copy-start.6
  47.4 0.7 copy-start.7
  48.1 26.9 %copy-start.9 = (f32[8]{0:T(128)S(1)}, f32[8]{0:T(128)}, u32[]{:S(2)}) copy-start(f32[8]{0:T(128)} %gains_ref.1) | copy-start | bytes 100
  48.1 26.9 %copy-start.10 = (f32[8]{0:T(128)S(1)}, f32[8]{0:T(128)}, u32[]{:S(2)}) copy-start(f32[8]{0:T(128)} %rates_ref.1) | copy-start | bytes 100
  50.4 43.6 %copy-start.3 = (f32[128,128]{1,0:T(8,128)S(1)}, f32[128,128]{1,0:T(8,128)}, u32[]{:S(2)}) copy-start(f32[128,128]{1,0:T(8,128)} %height_ref.5) | copy-start | bytes 196612
  94.0 1.6 %copy-start = (f32[4352,128]{1,0:T(8,128)S(1)}, f32[4352,128]{1,0:T(8,128)}, u32[]{:S(2)}) copy-start(f32[4352,128]{1,0:T(8,128)} %all-gather.3.cloned.1.call-done) | copy-start | bytes 6684676
Sparse Core Ops, SparseCore 0:
  10.1 75.0 all-gather.2

commit v2 on v1

v2 whole, which is shorter than its diff:
```python
import functools

import jax
import jax.numpy as jnp
from jax import lax
from jax.experimental import pallas as pl
from jax.experimental.pallas import tpu as pltpu
from jax.sharding import PartitionSpec as P

CHANNELS = 8
TAPS = 33
HALF = TAPS // 2
SIDE = 128
ROWS = 16
COLS = 32
PEERS = COLS // 2
SUB = SIDE // ROWS
MIXED = CHANNELS - 1
F32 = jnp.float32
BF16 = jnp.bfloat16
VMEM = pl.BlockSpec(memory_space=pltpu.VMEM)
SMEM = pl.BlockSpec(memory_space=pltpu.SMEM)
ANY = pl.BlockSpec(memory_space=pl.ANY)
HBM = pl.BlockSpec(memory_space=pltpu.HBM)
PARAMS = pltpu.CompilerParams(vmem_limit_bytes=24 * 1024 * 1024)


def reach(channel):
    return max(1, 2**channel * HALF // SIDE)


def blocks(channel):
    return 2 * reach(channel) + 1


def split(values):
    high = values.astype(BF16)
    low = (values - high.astype(F32)).astype(BF16)
    return high, low


def pair_rows(first, second):
    return jnp.concatenate(
        [first.reshape(ROWS, SUB, SIDE), second.reshape(ROWS, SUB, SIDE)], axis=1
    )


def unpair_rows(pairs):
    values = pairs.astype(F32)
    return (
        values[:, :SUB, :].reshape(SIDE, SIDE),
        values[:, SUB:, :].reshape(SIDE, SIDE),
    )


def scaled(values, scale):
    return (values.reshape(ROWS, SUB, SIDE) * scale).reshape(SIDE, SIDE)


def fetch(sources, targets, sem):
    copies = [
        pltpu.make_async_copy(source, target, sem.at[number])
        for number, (source, target) in enumerate(zip(sources, targets))
    ]
    for copy in copies:
        copy.start()
    for copy in copies:
        copy.wait()


def scatter_round(values, place):
    near = values.astype(BF16).astype(F32)
    step = (near * (1.0 + 0.7 / 128)).astype(BF16).astype(F32) - near
    row = lax.broadcasted_iota(jnp.int32, values.shape, 0).astype(F32)
    column = lax.broadcasted_iota(jnp.int32, values.shape, 1).astype(F32)
    mixed = row * 0.7548777 + column * 0.5698403 + place.astype(F32) * 0.6180340
    return (values + step * (mixed - jnp.floor(mixed) - 0.5)).astype(BF16)


def source_kernel(place_ref, region_ref, fill_in, height_in, density_in, out_ref, *scratch):
    fill_ref, height_ref, density_ref, sem = scratch
    fetch((fill_in, height_in, density_in), (fill_ref, height_ref, density_ref), sem)
    fill = fill_ref[region_ref[0, 0]]
    height = height_ref[...]
    source = (density_ref[...] + fill) * height
    turned = source.T.astype(BF16)
    rounded = scatter_round(height, place_ref[0])
    for peer in range(PEERS):
        out_ref[peer, :SIDE, :] = turned
        out_ref[peer, SIDE:, :] = rounded


def toeplitz(taps_ref, channel, direction, merged):
    width = (blocks(channel) + 1) * SIDE
    lane = lax.broadcasted_iota(jnp.int32, (1, SIDE), 1)
    parts = [jnp.zeros((1, SIDE), F32) for _ in range(width // SIDE)]
    for position in range(TAPS):
        value = taps_ref[channel, position]
        if merged and position == 0:
            continue
        if merged and position == TAPS - 1:
            value = value + taps_ref[channel, 0]
        place = reach(channel) * SIDE + direction * (position - HALF) * 2**channel
        part, inside = divmod(place, SIDE)
        parts[part] = jnp.where(lane == inside, value, parts[part])
    base = jnp.concatenate(parts, axis=1).astype(BF16).astype(F32)
    spread = jnp.broadcast_to(base, (SIDE, width))
    rolled = pltpu.roll(spread, 0, 1, stride=1, stride_axis=0)
    return rolled[:, : blocks(channel) * SIDE].astype(BF16)


def fill_tables(taps_ref, outs, last_ref, direction, merged):
    for channel in range(MIXED):
        outs[channel][...] = toeplitz(taps_ref, channel, direction, merged and channel == 6)
    steps = last_ref.shape[0]
    for step in range(steps):
        places = [t for t in range(TAPS) if (direction * (t - HALF) + HALF - step) % steps == 0]
        value = taps_ref[MIXED, places[0]]
        for place in places[1:]:
            value = value + taps_ref[MIXED, place]
        last_ref[step] = jnp.full((SUB, SIDE), value, F32).astype(BF16).astype(F32)


def tables_kernel(col_in, row_in, gains_in, rates_in, after_ref, *refs):
    scales_ref, col_ref, row_ref, gains_ref, rates_ref, sem = refs[2 * MIXED + 2 :]
    fetch(
        (col_in, row_in, gains_in, rates_in), (col_ref, row_ref, gains_ref, rates_ref), sem
    )
    for number in range(CHANNELS):
        scales_ref[number] = jnp.full((SUB, SIDE), gains_ref[number], F32)
        scales_ref[CHANNELS + number] = jnp.full((SUB, SIDE), rates_ref[number], F32)
    fill_tables(col_ref, refs[:MIXED], refs[MIXED], -1, False)
    fill_tables(row_ref, refs[MIXED + 1 : 2 * MIXED + 1], refs[2 * MIXED + 1], 1, True)


def smooth_kernel(place_ref, class_ref, own_ref, other_ref, height_in, target_in, last_ref, *refs):
    tables, out_ref = refs[:MIXED], refs[MIXED]
    window_ref, height_ref, target_ref, sem = refs[MIXED + 1 :]
    copies = [
        pltpu.make_async_copy(height_in, height_ref, sem.at[0]),
        pltpu.make_async_copy(target_in, target_ref, sem.at[1]),
    ]
    for copy in copies:
        copy.start()
    here = place_ref[0]
    last = jnp.zeros((SIDE, SIDE), F32)
    for step in range(COLS):
        block = lax.rem(here + (COLS - HALF + step), COLS) // 2
        chunk_ref = own_ref if step % 2 == 0 else other_ref
        values = chunk_ref[block, :SIDE, :]
        window_ref[step * SIDE : (step + 1) * SIDE, :] = values
        last = last + scaled(values.astype(F32), last_ref[step])
    smoothed = []
    for channel in range(MIXED):
        first = (HALF - reach(channel)) * SIDE
        smoothed.append(
            jnp.dot(
                tables[channel][...],
                window_ref[first : first + blocks(channel) * SIDE, :],
                preferred_element_type=F32,
            )
        )
    smoothed.append(last)
    for pair in range(CHANNELS // 2):
        out_ref[:, 16 * pair : 16 * pair + 16, :] = pair_rows(
            smoothed[2 * pair], smoothed[2 * pair + 1]
        ).astype(BF16)
    for copy in copies:
        copy.wait()
    away = (height_ref[...] - target_ref[...]).T
    high, low = split(away)
    out_ref[:, 64:80, :] = pair_rows(high.astype(F32), low.astype(F32)).astype(BF16)
    kind = class_ref[0, 0].astype(F32)
    out_ref[:, 80:, :] = jnp.full((ROWS, 16, SIDE), kind, F32).astype(BF16)


def rolled_rows(values, block_shift):
    shift = block_shift * SUB % SIDE
    if shift == 0:
        return values
    return jnp.concatenate([values[SIDE - shift :], values[: SIDE - shift]], axis=0)


def pressure_kernel(scales_ref, long_ref, last_ref, *refs):
    tables, out_ref, gain_ref = refs[:MIXED], refs[MIXED], refs[MIXED + 1]
    smoothed = []
    for pair in range(CHANNELS // 2):
        smoothed.extend(unpair_rows(long_ref[:, 16 * pair : 16 * pair + 16, :]))
    high, low = unpair_rows(long_ref[:, 64:80, :])
    away = high + low
    kind, _ = unpair_rows(long_ref[:, 80:96, :])
    kind = kind.reshape(ROWS, SUB, SIDE)
    rate = jnp.zeros((ROWS, SUB, SIDE), F32)
    for number in range(CHANNELS):
        rate = jnp.where(kind == float(number), scales_ref[CHANNELS + number], rate)
    rate = rate.reshape(SIDE, SIDE)

    pressure = jnp.zeros((SIDE, SIDE), F32)
    for channel in range(MIXED):
        spread = jnp.dot(
            smoothed[channel].astype(BF16), tables[channel][...], preferred_element_type=F32
        )
        total = None
        for block in range(blocks(channel)):
            term = rolled_rows(
                spread[:, block * SIDE : (block + 1) * SIDE], block - reach(channel)
            )
            total = term if total is None else total + term
        pressure = pressure + scaled(total, scales_ref[channel])
    total = jnp.zeros((SIDE, SIDE), F32)
    for step in range(ROWS):
        total = total + rolled_rows(scaled(smoothed[MIXED], last_ref[step]), step)
    pressure = pressure + scaled(total, scales_ref[MIXED])

    shifted = 1.0 + pressure
    decay = jnp.exp(-jnp.abs(shifted))
    removed = rate * (jnp.maximum(shifted, 0.0) + jnp.log1p(decay))
    slope = jnp.where(shifted >= 0, 1.0, decay) / (1.0 + decay)
    adjoint = (-(away - removed) * rate * slope / SIDE).astype(BF16)

    weighted = []
    gain_rows = []
    for channel in range(CHANNELS):
        total = jnp.zeros((SIDE, SIDE), F32)
        if channel < MIXED:
            for block in range(blocks(channel)):
                term = lax.dot_general(
                    adjoint,
                    tables[channel][:, block * SIDE : (block + 1) * SIDE],
                    (((1,), (1,)), ((), ())),
                    preferred_element_type=F32,
                )
                total = total + rolled_rows(term, reach(channel) - block)
        else:
            wide = adjoint.astype(F32)
            for step in range(ROWS):
                total = total + rolled_rows(scaled(wide, last_ref[step]), -step)
        gain_rows.append(jnp.sum(total * smoothed[channel], axis=0, keepdims=True))
        weighted.append(scaled(total, scales_ref[channel]))
    for pair in range(CHANNELS // 2):
        out_ref[:, 16 * pair : 16 * pair + 16, :] = pair_rows(
            weighted[2 * pair], weighted[2 * pair + 1]
        ).astype(BF16)
    high, low = split(removed)
    out_ref[:, 64:, :] = pair_rows(high.astype(F32), low.astype(F32)).astype(BF16)
    gain_ref[...] = jnp.concatenate(gain_rows, axis=0)


def gradient_kernel(
    place_ref, region_ref, back_ref, own_ref, other_ref, gain_ref, height_in, last_ref, *refs
):
    tables, new_ref, sums_ref = refs[:MIXED], refs[MIXED], refs[MIXED + 1]
    height_ref, sem = refs[MIXED + 2 :]
    copy = pltpu.make_async_copy(height_in, height_ref, sem.at[0])
    copy.start()
    weighted = []
    for pair in range(CHANNELS // 2):
        weighted.extend(unpair_rows(back_ref[:, 16 * pair : 16 * pair + 16, :]))
    turned = weighted[MIXED].T
    narrow = [weighted[channel].astype(BF16) for channel in range(MIXED)]
    here = place_ref[0]
    lane = lax.broadcasted_iota(jnp.int32, (1, SIDE), 1)
    line = jnp.zeros((1, SIDE), F32)
    for step in range(COLS):
        block = lax.rem(here + (COLS - HALF + step), COLS) // 2
        values = (own_ref if step % 2 == 0 else other_ref)[block, SIDE:, :]
        product = turned * values.astype(F32)
        product = jnp.sum(product.reshape(ROWS, SUB, SIDE), axis=0)
        terms = product * last_ref[step]
        ahead = step - HALF
        channels = [c for c in range(MIXED) if abs(ahead) <= reach(c)]
        for channel in channels:
            first = (ahead + reach(channel)) * SIDE
            cross = jnp.dot(narrow[channel], values, preferred_element_type=F32)
            taps = tables[channel][:, first : first + SIDE].astype(F32)
            terms = terms + jnp.sum((cross * taps).reshape(ROWS, SUB, SIDE), axis=0)
        total = jnp.sum(jnp.sum(terms, axis=0, keepdims=True), axis=1, keepdims=True)
        line = line + jnp.where(lane == step, total, 0.0)
    gain = jnp.sum(gain_ref[...], axis=1, keepdims=True)
    row = lax.broadcasted_iota(jnp.int32, (SUB, SIDE), 0)
    wide_lane = lax.broadcasted_iota(jnp.int32, (SUB, SIDE), 1)
    gain = jnp.sum(jnp.where(row + COLS == wide_lane, gain, 0.0), axis=0, keepdims=True)
    region = region_ref[0, 0].astype(F32)
    line = line + gain + jnp.where(lane == COLS + SUB, region, 0.0)
    for peer in range(COLS):
        sums_ref[peer] = line
    high, low = unpair_rows(back_ref[:, 64:80, :])
    copy.wait()
    new_ref[...] = height_ref[...] - (high + low).T


def regions_kernel(place_ref, lines_ref, out_ref):
    lines = lines_ref[...].reshape(COLS, SIDE)
    sender = lax.broadcasted_iota(jnp.int32, (COLS, SIDE), 0)
    lane = lax.broadcasted_iota(jnp.int32, (COLS, SIDE), 1)
    sums = jnp.where(lane < COLS, lines, 0.0)
    region = jnp.sum(jnp.where(lane == COLS + SUB, lines, 0.0), axis=1, keepdims=True)
    gain = jnp.sum(jnp.where((lane >= COLS) & (lane < COLS + SUB), lines, 0.0), axis=0, keepdims=True)
    fill = jnp.zeros((1, SIDE), F32)
    for block in range(COLS):
        held = jnp.sum(jnp.where(lane == lax.rem(block + HALF - sender + COLS, COLS), sums, 0.0))
        fill = fill + jnp.where(region[block : block + 1] == lane[:1].astype(F32), held, 0.0)
    both = jnp.concatenate([fill, gain], axis=0)
    for peer in range(ROWS):
        out_ref[peer] = both


def total_kernel(sums_ref, fill_ref, gain_ref):
    total = jnp.sum(sums_ref[...], axis=0)
    fill_ref[...] = total[0]
    gain_ref[...] = total[1, COLS : COLS + CHANNELS]


def shape(*dims, dtype=F32):
    return jax.ShapeDtypeStruct(dims, dtype)


def shards(
    height,
    density,
    target,
    region_of_block,
    class_of_block,
    fill_level,
    rates,
    col_taps,
    row_taps,
    gains,
):
    place = lax.axis_index("col").astype(jnp.int32).reshape(1)
    copies = pl.pallas_call(
        source_kernel,
        out_shape=shape(PEERS, 2 * SIDE, SIDE, dtype=BF16),
        in_specs=[SMEM, SMEM, HBM, HBM, HBM],
        out_specs=VMEM,
        scratch_shapes=[
            pltpu.SMEM((SIDE,), F32),
            pltpu.VMEM((SIDE, SIDE), F32),
            pltpu.VMEM((SIDE, SIDE), F32),
            pltpu.SemaphoreType.DMA((3,)),
        ],
        compiler_params=pltpu.CompilerParams(vmem_limit_bytes=60 * 1024 * 1024),
        name="source",
    )(place, region_of_block, fill_level, height, density)
    groups = [[2 * block + core for block in range(PEERS)] for core in range(2)]
    own = lax.all_to_all(copies, "col", 0, 0, axis_index_groups=groups, tiled=True)
    other = lax.ppermute(own, "col", [(block, block ^ 1) for block in range(COLS)])
    table_shapes = [shape(SIDE, blocks(c) * SIDE, dtype=BF16) for c in range(MIXED)]
    made = pl.pallas_call(
        tables_kernel,
        out_shape=table_shapes
        + [shape(COLS, SUB, SIDE)]
        + table_shapes
        + [shape(ROWS, SUB, SIDE), shape(2 * CHANNELS, SUB, SIDE)],
        in_specs=[HBM] * 4 + [ANY],
        out_specs=[VMEM] * (2 * MIXED + 3),
        scratch_shapes=[
            pltpu.SMEM((CHANNELS, TAPS), F32),
            pltpu.SMEM((CHANNELS, TAPS), F32),
            pltpu.SMEM((CHANNELS,), F32),
            pltpu.SMEM((CHANNELS,), F32),
            pltpu.SemaphoreType.DMA((4,)),
        ],
        compiler_params=PARAMS,
        cost_estimate=pl.CostEstimate(flops=4000000, bytes_accessed=4000000, transcendentals=0),
        name="tables",
    )(col_taps, row_taps, gains, rates, own)
    col_tables, col_last = made[:MIXED], made[MIXED]
    row_tables, row_last = made[MIXED + 1 : 2 * MIXED + 1], made[2 * MIXED + 1]
    scales = made[2 * MIXED + 2]

    smoothed = pl.pallas_call(
        smooth_kernel,
        out_shape=shape(ROWS, 96, SIDE, dtype=BF16),
        in_specs=[SMEM, SMEM, VMEM, VMEM, HBM, HBM] + [VMEM] * (1 + MIXED),
        out_specs=VMEM,
        scratch_shapes=[
            pltpu.VMEM((COLS * SIDE, SIDE), BF16),
            pltpu.VMEM((SIDE, SIDE), F32),
            pltpu.VMEM((SIDE, SIDE), F32),
            pltpu.SemaphoreType.DMA((2,)),
        ],
        compiler_params=PARAMS,
        name="smooth",
    )(place, class_of_block, own, other, height, target, col_last, *col_tables)
    long = lax.all_to_all(smoothed, "row", 0, 0, tiled=True)

    back, gain_part = pl.pallas_call(
        pressure_kernel,
        out_shape=[shape(ROWS, 80, SIDE, dtype=BF16), shape(CHANNELS, SIDE)],
        in_specs=[VMEM] * (3 + MIXED),
        out_specs=[VMEM, VMEM],
        compiler_params=PARAMS,
        name="pressure",
    )(scales, long, row_last, *row_tables)
    tile = lax.all_to_all(back, "row", 0, 0, tiled=True)
    new_height, lines = pl.pallas_call(
        gradient_kernel,
        out_shape=[shape(SIDE, SIDE), shape(COLS, 1, SIDE)],
        in_specs=[SMEM, SMEM] + [VMEM] * 4 + [HBM] + [VMEM] * (1 + MIXED),
        out_specs=[VMEM, VMEM],
        scratch_shapes=[pltpu.VMEM((SIDE, SIDE), F32), pltpu.SemaphoreType.DMA((1,))],
        compiler_params=PARAMS,
        name="gradient",
    )(place, region_of_block, tile, own, other, gain_part, height, col_last, *col_tables)
    by_col = lax.all_to_all(lines, "col", 0, 0, tiled=True)
    sums = pl.pallas_call(
        regions_kernel,
        out_shape=shape(ROWS, 2, SIDE),
        in_specs=[SMEM, VMEM],
        out_specs=VMEM,
        compiler_params=PARAMS,
        name="regions",
    )(place, by_col)
    by_row = lax.all_to_all(sums, "row", 0, 0, tiled=True)
    fill_grad, gain_grad = pl.pallas_call(
        total_kernel,
        out_shape=[shape(SIDE), shape(CHANNELS)],
        in_specs=[VMEM],
        out_specs=[VMEM, VMEM],
        compiler_params=PARAMS,
        name="total",
    )(by_row)
    return new_height, gain_grad, fill_grad


def solution(mesh):
    cells = P("row", "col")
    in_specs = (cells,) * 5 + (P(),) * 5
    out_specs = (cells, P(), P())
    return jax.shard_map(shards, mesh=mesh, in_specs=in_specs, out_specs=out_specs, check_vma=False)
```

time: 132 us -> 120 us (0.909)
  between operations: 15.4 us -> 2.07 us
  blocking collectives: 93 us -> 104 us
  local copies, waits for them, and re-layouts: 9.53 us -> 0.03 us
  Pallas kernels: 6.8 us -> 8.68 us
    all_to_all x1, blocking collectives: 25.8 us -> 36.9 us  [shards(): lax.all_to_all(copies, 'col', 0, 0, axis_index_groups=groups, tiled=True)]
    unnamed x22 -> x12, local copies, waits for them, and re-layouts: 7.02 us -> 0.03 us
    pallas_call x2 -> x4, Pallas kernels: 2.2 us -> 4.41 us  [the longest x1 2.01 us: shards(): pl.pallas_call(source_kernel, out_shape=shape(PEERS, 2 * SIDE, SIDE, dtyp...]
    concatenate x1 -> x0, local copies, waits for them, and re-layouts: 1.48 us -> none  [shards(): marked = jnp.concatenate([height, marks], axis=0)]
  transfers between devices with their start and end apart: 2 -> 1, of which waited for: 0 -> 0; matrix products, arithmetic and copies ran while one was open for 0% -> 0% of each run, Pallas kernels for 4% -> 1%
where the time goes in v2:
time: 120 us
  blocking collectives  104 us (87%)
  Pallas kernels  8.68 us (7%)
  starting transfers between devices  4.95 us (4%)
  between operations  2.07 us (2%)
    all_to_all x1, blocking collectives, shards(): lax.all_to_all(copies, 'col', 0, 0, axis_index_groups=groups, tiled=True)  36.9 us
    all_to_all x1, blocking collectives, shards(): long = lax.all_to_all(smoothed, 'row', 0, 0, tiled=True)  23.9 us
    all_to_all x1, blocking collectives, shards(): tile = lax.all_to_all(back, 'row', 0, 0, tiled=True)  17.4 us
    all_to_all x1, blocking collectives, shards(): by_col = lax.all_to_all(lines, 'col', 0, 0, tiled=True)  14 us
    all_to_all x1, blocking collectives, shards(): by_row = lax.all_to_all(sums, 'row', 0, 0, tiled=True)  11.6 us
    ppermute x1, starting transfers between devices, shards(): lax.ppermute(own, 'col', [(block, block ^ 1) for block in range(COLS)])  4.95 us
  transfers between devices with their start and end apart: 1, of which 0 were waited for; matrix products, arithmetic and copies ran while one was open for 0% of the time, Pallas kernels for 1%

profile of v2, /device:TPU:1, one launch (start us, length us, event | category | flops | bytes accessed | tf_op | source)
XLA Modules:
  0.0 119.6 jit_solution(18072500018822789872)
XLA Ops:
  1.3 2.0 %source.1 = bf16[16,256,128]{2,1,0:T(8,128)(2,1)} custom-call(s32[1]{0:T(128)} %bitcast.place_ref, s32[1,1]{1,0:T(1,128)S(6)} %copy.13.region_ref, f32[128]{0:T(128)} %fill_in.1, f32[128,128]{1,0:T(8,128)} %height_in.5, f32[128,128]{1,0:T(8,128)} %density_in.1), custom_call_target="tpu_custom_call" | custom-call | tf_op jit(solution)/shard_map/source/pallas_call | solution.py:331
  3.3 0.0 copy-start.2
  3.3 0.0 copy-start.3
  3.3 36.9 %all_to_all.25.after_ref.own_ref = bf16[16,256,128]{2,1,0:T(8,128)(2,1)S(1)} all-to-all(bf16[16,256,128]{2,1,0:T(8,128)(2,1)} %source.1), channel_id=1, replica_groups={{0,2,4,6,8,10,12,14,16,18,20,22,24,26,28,30},{1,3,5,7,9,11,13,15,17,19,..., dimensions={0} | all-to-all | bytes 2097152 | tf_op jit(solution)/shard_map/all_to_all | solution.py:346
  40.2 0.0 copy-start.4
  40.2 0.0 copy-start.5
  40.2 5.0 %collective-permute-start = (bf16[16,256,128]{2,1,0:T(8,128)(2,1)S(1)}, bf16[16,256,128]{2,1,0:T(8,128)(2,1)S(1)}, u32[]{:S(2)}, u32[]{:S(2)}) collective-permute-start(bf16[16,256,128]{2,1,0:T(8,128)(2,1)S(1)} %all_to_all.25.after_ref.own_ref), channel_id=1, source_target_pairs={{0,1},{1,0},{2,3},{3,2},{4,5},{5,4},{6,7},{7,6},{8,9},{9,8},{10,11... | collective-permute-start | bytes 3145736 | tf_op jit(solution)/shard_map/ppermute | solution.py:347
  45.8 0.0 copy-done.2
  45.8 0.0 copy-done.3
  45.8 0.0 copy-done.4
  45.8 0.0 copy-done.5
  45.8 0.0 copy-start
  45.9 0.0 copy-start.1
  45.9 1.6 %tables.1 = (bf16[128,384]{1,0:T(8,128)(2,1)S(1)}, bf16[128,384]{1,0:T(8,128)(2,1)S(1)}, bf16[128,384]{1,0:T(8,128)(2,1)S(1)}, bf16[128,384]{1,0:T(8,128)(2,1)S(...) custom-call(f32[8,33]{1,0:T(8,128)S(1)} %copy-done.2, ...), custom_call_target="tpu_custom_call" | custom-call | flops 4000000 | bytes 4000000 | tf_op jit(solution)/shard_map/tables/pallas_call | solution.py:349
  47.4 0.0 collective-permute-done.other_ref
  47.4 0.0 copy-done
  47.4 0.0 copy-done.1
  47.5 1.0 smooth.1
  48.5 23.9 %all_to_all.26.long_ref = bf16[16,96,128]{2,1,0:T(8,128)(2,1)S(1)} all-to-all(bf16[16,96,128]{2,1,0:T(8,128)(2,1)S(1)} %smooth.1), channel_id=1, replica_groups=mesh['row'=16,'col'=32] {'row'}, dimensions={0} | all-to-all | bytes 786432 | tf_op jit(solution)/shard_map/all_to_all | solution.py:386
  72.4 1.7 %pressure.1 = (bf16[16,80,128]{2,1,0:T(8,128)(2,1)S(1)}, f32[8,128]{1,0:T(8,128)S(1)}) custom-call(f32[16,8,128]{2,1,0:T(8,128)S(1)} %get-tuple-element.26.scales_ref, bf16[16,96,128]{2,1,0:T(8,128)(2,1)S(1)} %all_to_all.26.long_ref, f32[16,8,128]{2,1,0:T(8,128)S(1)} %get-tuple-element.35.last_ref, bf16[128,384]{1,0:T(8,128)(2,1)S(1)} %get-tuple-element.36.refs_0_, ...), custom_call_target="tpu_custom_call" | custom-call | tf_op jit(solution)/shard_map/pressure/pallas_call | solution.py:388
  74.1 17.4 %all_to_all.27.back_ref = bf16[16,80,128]{2,1,0:T(8,128)(2,1)S(1)} all-to-all(bf16[16,80,128]{2,1,0:T(8,128)(2,1)S(1)} %get-tuple-element.43), channel_id=1, replica_groups=mesh['row'=16,'col'=32] {'row'}, dimensions={0} | all-to-all | bytes 655360 | tf_op jit(solution)/shard_map/all_to_all | solution.py:396
  91.6 1.5 %gradient.1 = (f32[128,128]{1,0:T(8,128)}, f32[32,1,128]{2,1,0:T(1,128)S(1)}) custom-call(s32[1]{0:T(128)} %bitcast.place_ref, s32[1,1]{1,0:T(1,128)S(6)} %copy.13.region_ref, bf16[16,80,128]{2,1,0:T(8,128)(2,1)S(1)} %all_to_all.27.back_ref, bf16[16,256,128]{2,1,0:T(8,128)(2,1)S(1)} %all_to_all.25.after_ref.own_ref, ...), custom_call_target="tpu_custom_call" | custom-call | tf_op jit(solution)/shard_map/gradient/pallas_call | solution.py:397
  93.1 14.0 %all_to_all.28.lines_ref = f32[32,1,128]{2,1,0:T(1,128)S(1)} all-to-all(f32[32,1,128]{2,1,0:T(1,128)S(1)} %get-tuple-element.46), channel_id=1, replica_groups=mesh['row'=16,'col'=32] {'col'}, dimensions={0} | all-to-all | bytes 32768 | tf_op jit(solution)/shard_map/all_to_all | solution.py:406
  107.1 0.3 regions.1
  107.4 11.6 %all_to_all.29.sums_ref = f32[16,2,128]{2,1,0:T(2,128)S(1)} all-to-all(f32[16,2,128]{2,1,0:T(2,128)S(1)} %regions.1), channel_id=1, replica_groups=mesh['row'=16,'col'=32] {'row'}, dimensions={0} | all-to-all | bytes 32768 | tf_op jit(solution)/shard_map/all_to_all | solution.py:415
  119.0 0.6 total.1
Async XLA Ops:
  3.3 42.5 %copy-start.2 = (f32[8,33]{1,0:T(8,128)S(1)}, f32[8,33]{1,0:T(8,128)}, u32[]{:S(2)}) copy-start(f32[8,33]{1,0:T(8,128)} %col_in.1) | copy-start | bytes 3172
  3.3 42.5 %copy-start.3 = (f32[8,33]{1,0:T(8,128)S(1)}, f32[8,33]{1,0:T(8,128)}, u32[]{:S(2)}) copy-start(f32[8,33]{1,0:T(8,128)} %row_in.1) | copy-start | bytes 3172
  40.2 5.6 %copy-start.4 = (f32[8]{0:T(128)S(1)}, f32[8]{0:T(128)}, u32[]{:S(2)}) copy-start(f32[8]{0:T(128)} %gains_in.1) | copy-start | bytes 100
  40.2 5.6 %copy-start.5 = (f32[8]{0:T(128)S(1)}, f32[8]{0:T(128)}, u32[]{:S(2)}) copy-start(f32[8]{0:T(128)} %rates_in.1) | copy-start | bytes 100
  40.2 7.2 %collective-permute-start = (bf16[16,256,128]{2,1,0:T(8,128)(2,1)S(1)}, bf16[16,256,128]{2,1,0:T(8,128)(2,1)S(1)}, u32[]{:S(2)}, u32[]{:S(2)}) collective-permute-start(bf16[16,256,128]{2,1,0:T(8,128)(2,1)S(1)} %all_to_all.25.after_ref.own_ref), channel_id=1, source_target_pairs={{0,1},{1,0},{2,3},{3,2},{4,5},{5,4},{6,7},{7,6},{8,9},{9,8},{10,11... | collective-permute-start | bytes 3145736 | tf_op jit(solution)/shard_map/ppermute | solution.py:347
  45.8 1.6 %copy-start = (f32[128,128]{1,0:T(8,128)S(1)}, f32[128,128]{1,0:T(8,128)}, u32[]{:S(2)}) copy-start(f32[128,128]{1,0:T(8,128)} %height_in.5) | copy-start | bytes 196612
  45.9 1.6 %copy-start.1 = (f32[128,128]{1,0:T(8,128)S(1)}, f32[128,128]{1,0:T(8,128)}, u32[]{:S(2)}) copy-start(f32[128,128]{1,0:T(8,128)} %target_in.1) | copy-start | bytes 196612

commit v3 on v2

--- a/solution.py
+++ b/solution.py
@@ -169,9 +169,11 @@
         copy.wait()
     away = (height_ref[...] - target_ref[...]).T
     high, low = split(away)
-    out_ref[:, 64:80, :] = pair_rows(high.astype(F32), low.astype(F32)).astype(BF16)
-    kind = class_ref[0, 0].astype(F32)
-    out_ref[:, 80:, :] = jnp.full((ROWS, 16, SIDE), kind, F32).astype(BF16)
+    row = lax.broadcasted_iota(jnp.int32, (SIDE, SIDE), 0)
+    lane = lax.broadcasted_iota(jnp.int32, (SIDE, SIDE), 1)
+    first = (row % SUB == 0) & (lane == 0)
+    low = jnp.where(first, class_ref[0, 0].astype(F32), low.astype(F32))
+    out_ref[:, 64:, :] = pair_rows(high.astype(F32), low).astype(BF16)
 
 
 def rolled_rows(values, block_shift):
@@ -186,10 +188,13 @@
     smoothed = []
     for pair in range(CHANNELS // 2):
         smoothed.extend(unpair_rows(long_ref[:, 16 * pair : 16 * pair + 16, :]))
-    high, low = unpair_rows(long_ref[:, 64:80, :])
-    away = high + low
-    kind, _ = unpair_rows(long_ref[:, 80:96, :])
-    kind = kind.reshape(ROWS, SUB, SIDE)
+    high, low = unpair_rows(long_ref[:, 64:, :])
+    low = low.reshape(ROWS, SUB, SIDE)
+    row = lax.broadcasted_iota(jnp.int32, (ROWS, SUB, SIDE), 1)
+    lane = lax.broadcasted_iota(jnp.int32, (ROWS, SUB, SIDE), 2)
+    first = (row == 0) & (lane == 0)
+    kind = jnp.max(jnp.where(first, low, 0.0), axis=(1, 2), keepdims=True)
+    away = high + jnp.where(first, 0.0, low).reshape(SIDE, SIDE)
     rate = jnp.zeros((ROWS, SUB, SIDE), F32)
     for number in range(CHANNELS):
         rate = jnp.where(kind == float(number), scales_ref[CHANNELS + number], rate)
@@ -371,7 +376,7 @@
 
     smoothed = pl.pallas_call(
         smooth_kernel,
-        out_shape=shape(ROWS, 96, SIDE, dtype=BF16),
+        out_shape=shape(ROWS, 80, SIDE, dtype=BF16),
         in_specs=[SMEM, SMEM, VMEM, VMEM, HBM, HBM] + [VMEM] * (1 + MIXED),
         out_specs=VMEM,
         scratch_shapes=[

time: 120 us -> 119 us (level)
  blocking collectives: 104 us -> 102 us
where the time goes in v3:
time: 119 us; the launch traced here: 118 us
  blocking collectives  102 us (86%)
  Pallas kernels  8.67 us (7%)
  starting transfers between devices  4.95 us (4%)
  between operations  2.07 us (2%)
    all_to_all x1, blocking collectives, shards(): lax.all_to_all(copies, 'col', 0, 0, axis_index_groups=groups, tiled=True)  36.9 us
    all_to_all x1, blocking collectives, shards(): long = lax.all_to_all(smoothed, 'row', 0, 0, tiled=True)  22.8 us
    all_to_all x1, blocking collectives, shards(): tile = lax.all_to_all(back, 'row', 0, 0, tiled=True)  17.2 us
    all_to_all x1, blocking collectives, shards(): by_col = lax.all_to_all(lines, 'col', 0, 0, tiled=True)  14 us
    all_to_all x1, blocking collectives, shards(): by_row = lax.all_to_all(sums, 'row', 0, 0, tiled=True)  11.6 us
    ppermute x1, starting transfers between devices, shards(): lax.ppermute(own, 'col', [(block, block ^ 1) for block in range(COLS)])  4.95 us
  transfers between devices with their start and end apart: 1, of which 0 were waited for; matrix products, arithmetic and copies ran while one was open for 0% of the time, Pallas kernels for 1%

profile of v3, /device:TPU:1, one launch (start us, length us, event | category | flops | bytes accessed | tf_op | source)
XLA Modules:
  0.0 118.2 jit_solution(13930127183218534117)
XLA Ops:
  1.3 2.0 %source.1 = bf16[16,256,128]{2,1,0:T(8,128)(2,1)} custom-call(s32[1]{0:T(128)} %bitcast.place_ref, s32[1,1]{1,0:T(1,128)S(6)} %copy.13.region_ref, f32[128]{0:T(128)} %fill_in.1, f32[128,128]{1,0:T(8,128)} %height_in.5, f32[128,128]{1,0:T(8,128)} %density_in.1), custom_call_target="tpu_custom_call" | custom-call | tf_op jit(solution)/shard_map/source/pallas_call | solution.py:336
  3.3 0.0 copy-start.2
  3.3 0.0 copy-start.3
  3.3 36.9 %all_to_all.25.after_ref.own_ref = bf16[16,256,128]{2,1,0:T(8,128)(2,1)S(1)} all-to-all(bf16[16,256,128]{2,1,0:T(8,128)(2,1)} %source.1), channel_id=1, replica_groups={{0,2,4,6,8,10,12,14,16,18,20,22,24,26,28,30},{1,3,5,7,9,11,13,15,17,19,..., dimensions={0} | all-to-all | bytes 2097152 | tf_op jit(solution)/shard_map/all_to_all | solution.py:351
  40.2 0.0 copy-start.4
  40.2 0.0 copy-start.5
  40.2 5.0 %collective-permute-start = (bf16[16,256,128]{2,1,0:T(8,128)(2,1)S(1)}, bf16[16,256,128]{2,1,0:T(8,128)(2,1)S(1)}, u32[]{:S(2)}, u32[]{:S(2)}) collective-permute-start(bf16[16,256,128]{2,1,0:T(8,128)(2,1)S(1)} %all_to_all.25.after_ref.own_ref), channel_id=1, source_target_pairs={{0,1},{1,0},{2,3},{3,2},{4,5},{5,4},{6,7},{7,6},{8,9},{9,8},{10,11... | collective-permute-start | bytes 3145736 | tf_op jit(solution)/shard_map/ppermute | solution.py:352
  45.8 0.0 copy-done.2
  45.8 0.0 copy-done.3
  45.8 0.0 copy-done.4
  45.8 0.0 copy-done.5
  45.8 0.0 copy-start
  45.9 0.0 copy-start.1
  45.9 1.6 %tables.1 = (bf16[128,384]{1,0:T(8,128)(2,1)S(1)}, bf16[128,384]{1,0:T(8,128)(2,1)S(1)}, bf16[128,384]{1,0:T(8,128)(2,1)S(1)}, bf16[128,384]{1,0:T(8,128)(2,1)S(...) custom-call(f32[8,33]{1,0:T(8,128)S(1)} %copy-done.2, ...), custom_call_target="tpu_custom_call" | custom-call | flops 4000000 | bytes 4000000 | tf_op jit(solution)/shard_map/tables/pallas_call | solution.py:354
  47.4 0.0 collective-permute-done.other_ref
  47.4 0.0 copy-done
  47.4 0.0 copy-done.1
  47.5 1.0 smooth.1
  48.5 22.8 %all_to_all.26.long_ref = bf16[16,80,128]{2,1,0:T(8,128)(2,1)S(1)} all-to-all(bf16[16,80,128]{2,1,0:T(8,128)(2,1)S(1)} %smooth.1), channel_id=1, replica_groups=mesh['row'=16,'col'=32] {'row'}, dimensions={0} | all-to-all | bytes 655360 | tf_op jit(solution)/shard_map/all_to_all | solution.py:391
  71.3 1.7 %pressure.1 = (bf16[16,80,128]{2,1,0:T(8,128)(2,1)S(1)}, f32[8,128]{1,0:T(8,128)S(1)}) custom-call(f32[16,8,128]{2,1,0:T(8,128)S(1)} %get-tuple-element.26.scales_ref, bf16[16,80,128]{2,1,0:T(8,128)(2,1)S(1)} %all_to_all.26.long_ref, f32[16,8,128]{2,1,0:T(8,128)S(1)} %get-tuple-element.35.last_ref, bf16[128,384]{1,0:T(8,128)(2,1)S(1)} %get-tuple-element.36.refs_0_, ...), custom_call_target="tpu_custom_call" | custom-call | tf_op jit(solution)/shard_map/pressure/pallas_call | solution.py:393
  73.0 17.2 %all_to_all.27.back_ref = bf16[16,80,128]{2,1,0:T(8,128)(2,1)S(1)} all-to-all(bf16[16,80,128]{2,1,0:T(8,128)(2,1)S(1)} %get-tuple-element.43), channel_id=1, replica_groups=mesh['row'=16,'col'=32] {'row'}, dimensions={0} | all-to-all | bytes 655360 | tf_op jit(solution)/shard_map/all_to_all | solution.py:401
  90.2 1.5 %gradient.1 = (f32[128,128]{1,0:T(8,128)}, f32[32,1,128]{2,1,0:T(1,128)S(1)}) custom-call(s32[1]{0:T(128)} %bitcast.place_ref, s32[1,1]{1,0:T(1,128)S(6)} %copy.13.region_ref, bf16[16,80,128]{2,1,0:T(8,128)(2,1)S(1)} %all_to_all.27.back_ref, bf16[16,256,128]{2,1,0:T(8,128)(2,1)S(1)} %all_to_all.25.after_ref.own_ref, ...), custom_call_target="tpu_custom_call" | custom-call | tf_op jit(solution)/shard_map/gradient/pallas_call | solution.py:402
  91.7 14.0 %all_to_all.28.lines_ref = f32[32,1,128]{2,1,0:T(1,128)S(1)} all-to-all(f32[32,1,128]{2,1,0:T(1,128)S(1)} %get-tuple-element.46), channel_id=1, replica_groups=mesh['row'=16,'col'=32] {'col'}, dimensions={0} | all-to-all | bytes 32768 | tf_op jit(solution)/shard_map/all_to_all | solution.py:411
  105.7 0.3 regions.1
  106.0 11.6 %all_to_all.29.sums_ref = f32[16,2,128]{2,1,0:T(2,128)S(1)} all-to-all(f32[16,2,128]{2,1,0:T(2,128)S(1)} %regions.1), channel_id=1, replica_groups=mesh['row'=16,'col'=32] {'row'}, dimensions={0} | all-to-all | bytes 32768 | tf_op jit(solution)/shard_map/all_to_all | solution.py:420
  117.6 0.6 total.1
Async XLA Ops:
  3.3 42.5 %copy-start.2 = (f32[8,33]{1,0:T(8,128)S(1)}, f32[8,33]{1,0:T(8,128)}, u32[]{:S(2)}) copy-start(f32[8,33]{1,0:T(8,128)} %col_in.1) | copy-start | bytes 3172
  3.3 42.5 %copy-start.3 = (f32[8,33]{1,0:T(8,128)S(1)}, f32[8,33]{1,0:T(8,128)}, u32[]{:S(2)}) copy-start(f32[8,33]{1,0:T(8,128)} %row_in.1) | copy-start | bytes 3172
  40.2 5.6 %copy-start.4 = (f32[8]{0:T(128)S(1)}, f32[8]{0:T(128)}, u32[]{:S(2)}) copy-start(f32[8]{0:T(128)} %gains_in.1) | copy-start | bytes 100
  40.2 5.6 %copy-start.5 = (f32[8]{0:T(128)S(1)}, f32[8]{0:T(128)}, u32[]{:S(2)}) copy-start(f32[8]{0:T(128)} %rates_in.1) | copy-start | bytes 100
  40.2 7.2 %collective-permute-start = (bf16[16,256,128]{2,1,0:T(8,128)(2,1)S(1)}, bf16[16,256,128]{2,1,0:T(8,128)(2,1)S(1)}, u32[]{:S(2)}, u32[]{:S(2)}) collective-permute-start(bf16[16,256,128]{2,1,0:T(8,128)(2,1)S(1)} %all_to_all.25.after_ref.own_ref), channel_id=1, source_target_pairs={{0,1},{1,0},{2,3},{3,2},{4,5},{5,4},{6,7},{7,6},{8,9},{9,8},{10,11... | collective-permute-start | bytes 3145736 | tf_op jit(solution)/shard_map/ppermute | solution.py:352
  45.8 1.6 %copy-start = (f32[128,128]{1,0:T(8,128)S(1)}, f32[128,128]{1,0:T(8,128)}, u32[]{:S(2)}) copy-start(f32[128,128]{1,0:T(8,128)} %height_in.5) | copy-start | bytes 196612
  45.9 1.6 %copy-start.1 = (f32[128,128]{1,0:T(8,128)S(1)}, f32[128,128]{1,0:T(8,128)}, u32[]{:S(2)}) copy-start(f32[128,128]{1,0:T(8,128)} %target_in.1) | copy-start | bytes 196612

commit v4 on v3

--- a/solution.py
+++ b/solution.py
@@ -252,20 +252,16 @@
 
 
 def gradient_kernel(
-    place_ref, region_ref, back_ref, own_ref, other_ref, gain_ref, height_in, last_ref, *refs
+    place_ref, region_ref, back_ref, own_ref, other_ref, gain_ref, last_ref, *refs
 ):
-    tables, new_ref, sums_ref = refs[:MIXED], refs[MIXED], refs[MIXED + 1]
-    height_ref, sem = refs[MIXED + 2 :]
-    copy = pltpu.make_async_copy(height_in, height_ref, sem.at[0])
-    copy.start()
+    tables, sums_ref = refs[:MIXED], refs[MIXED]
     weighted = []
     for pair in range(CHANNELS // 2):
         weighted.extend(unpair_rows(back_ref[:, 16 * pair : 16 * pair + 16, :]))
     turned = weighted[MIXED].T
     narrow = [weighted[channel].astype(BF16) for channel in range(MIXED)]
     here = place_ref[0]
-    lane = lax.broadcasted_iota(jnp.int32, (1, SIDE), 1)
-    line = jnp.zeros((1, SIDE), F32)
+    parts = []
     for step in range(COLS):
         block = lax.rem(here + (COLS - HALF + step), COLS) // 2
         values = (own_ref if step % 2 == 0 else other_ref)[block, SIDE:, :]
@@ -279,41 +275,40 @@
             cross = jnp.dot(narrow[channel], values, preferred_element_type=F32)
             taps = tables[channel][:, first : first + SIDE].astype(F32)
             terms = terms + jnp.sum((cross * taps).reshape(ROWS, SUB, SIDE), axis=0)
-        total = jnp.sum(jnp.sum(terms, axis=0, keepdims=True), axis=1, keepdims=True)
-        line = line + jnp.where(lane == step, total, 0.0)
+        parts.append(terms)
+    total = jnp.sum(jnp.concatenate(parts, axis=0), axis=1, keepdims=True)
+    row = lax.broadcasted_iota(jnp.int32, (COLS * SUB, SIDE), 0)
+    lane = lax.broadcasted_iota(jnp.int32, (COLS * SUB, SIDE), 1)
+    block = lax.rem(here + HALF + row // SUB, COLS)
+    line = jnp.sum(jnp.where(lane == block, total, 0.0), axis=0, keepdims=True)
     gain = jnp.sum(gain_ref[...], axis=1, keepdims=True)
-    row = lax.broadcasted_iota(jnp.int32, (SUB, SIDE), 0)
-    wide_lane = lax.broadcasted_iota(jnp.int32, (SUB, SIDE), 1)
-    gain = jnp.sum(jnp.where(row + COLS == wide_lane, gain, 0.0), axis=0, keepdims=True)
+    gain = jnp.where(lane[:SUB] == COLS + row[:SUB], gain, 0.0)
     region = region_ref[0, 0].astype(F32)
-    line = line + gain + jnp.where(lane == COLS + SUB, region, 0.0)
+    line = line + jnp.sum(gain, axis=0, keepdims=True)
+    line = line + jnp.where(lane[:1] == 2 * COLS, region, 0.0)
     for peer in range(COLS):
         sums_ref[peer] = line
-    high, low = unpair_rows(back_ref[:, 64:80, :])
-    copy.wait()
-    new_ref[...] = height_ref[...] - (high + low).T
-
-
-def regions_kernel(place_ref, lines_ref, out_ref):
+
+
+def band_kernel(lines_ref, out_ref):
     lines = lines_ref[...].reshape(COLS, SIDE)
-    sender = lax.broadcasted_iota(jnp.int32, (COLS, SIDE), 0)
+    row = lax.broadcasted_iota(jnp.int32, (COLS, SIDE), 0)
     lane = lax.broadcasted_iota(jnp.int32, (COLS, SIDE), 1)
-    sums = jnp.where(lane < COLS, lines, 0.0)
-    region = jnp.sum(jnp.where(lane == COLS + SUB, lines, 0.0), axis=1, keepdims=True)
-    gain = jnp.sum(jnp.where((lane >= COLS) & (lane < COLS + SUB), lines, 0.0), axis=0, keepdims=True)
-    fill = jnp.zeros((1, SIDE), F32)
-    for block in range(COLS):
-        held = jnp.sum(jnp.where(lane == lax.rem(block + HALF - sender + COLS, COLS), sums, 0.0))
-        fill = fill + jnp.where(region[block : block + 1] == lane[:1].astype(F32), held, 0.0)
-    both = jnp.concatenate([fill, gain], axis=0)
+    band = jnp.sum(lines, axis=0, keepdims=True)
+    held = jnp.sum(jnp.where(lane == row, band, 0.0), axis=1, keepdims=True)
+    region = jnp.sum(jnp.where(lane == 2 * COLS, lines, 0.0), axis=1, keepdims=True)
+    fill = jnp.where(region == lane.astype(F32), held, 0.0)
+    both = jnp.concatenate([jnp.sum(fill, axis=0, keepdims=True), band], axis=0)
     for peer in range(ROWS):
         out_ref[peer] = both
 
 
-def total_kernel(sums_ref, fill_ref, gain_ref):
-    total = jnp.sum(sums_ref[...], axis=0)
+def total_kernel(bands_ref, back_ref, height_ref, new_ref, fill_ref, gain_ref):
+    total = jnp.sum(bands_ref[...], axis=0)
     fill_ref[...] = total[0]
     gain_ref[...] = total[1, COLS : COLS + CHANNELS]
+    high, low = unpair_rows(back_ref[:, 64:80, :])
+    new_ref[...] = height_ref[...] - (high + low).T
 
 
 def shape(*dims, dtype=F32):
@@ -399,33 +394,32 @@
         name="pressure",
     )(scales, long, row_last, *row_tables)
     tile = lax.all_to_all(back, "row", 0, 0, tiled=True)
-    new_height, lines = pl.pallas_call(
+    lines = pl.pallas_call(
         gradient_kernel,
-        out_shape=[shape(SIDE, SIDE), shape(COLS, 1, SIDE)],
-        in_specs=[SMEM, SMEM] + [VMEM] * 4 + [HBM] + [VMEM] * (1 + MIXED),
-        out_specs=[VMEM, VMEM],
-        scratch_shapes=[pltpu.VMEM((SIDE, SIDE), F32), pltpu.SemaphoreType.DMA((1,))],
+        out_shape=shape(COLS, 1, SIDE),
+        in_specs=[SMEM, SMEM] + [VMEM] * (5 + MIXED),
+        out_specs=VMEM,
         compiler_params=PARAMS,
         name="gradient",
-    )(place, region_of_block, tile, own, other, gain_part, height, col_last, *col_tables)
+    )(place, region_of_block, tile, own, other, gain_part, col_last, *col_tables)
     by_col = lax.all_to_all(lines, "col", 0, 0, tiled=True)
-    sums = pl.pallas_call(
-        regions_kernel,
+    bands = pl.pallas_call(
+        band_kernel,
         out_shape=shape(ROWS, 2, SIDE),
-        in_specs=[SMEM, VMEM],
+        in_specs=[VMEM],
         out_specs=VMEM,
         compiler_params=PARAMS,
-        name="regions",
-    )(place, by_col)
-    by_row = lax.all_to_all(sums, "row", 0, 0, tiled=True)
-    fill_grad, gain_grad = pl.pallas_call(
+        name="band",
+    )(by_col)
+    by_row = lax.all_to_all(bands, "row", 0, 0, tiled=True)
+    new_height, fill_grad, gain_grad = pl.pallas_call(
         total_kernel,
-        out_shape=[shape(SIDE), shape(CHANNELS)],
-        in_specs=[VMEM],
-        out_specs=[VMEM, VMEM],
+        out_shape=[shape(SIDE, SIDE), shape(SIDE), shape(CHANNELS)],
+        in_specs=[VMEM] * 3,
+        out_specs=[VMEM] * 3,
         compiler_params=PARAMS,
         name="total",
-    )(by_row)
+    )(by_row, tile, height)
     return new_height, gain_grad, fill_grad
 
 

time: 119 us -> 118 us (level)
  no operation moved by 1% of the time
where the time goes in v4:
time: 118 us; the launch traced here: 117 us
  blocking collectives  102 us (86%)
  Pallas kernels  7.85 us (7%)
  starting transfers between devices  4.95 us (4%)
  between operations  2.06 us (2%)
    all_to_all x1, blocking collectives, shards(): lax.all_to_all(copies, 'col', 0, 0, axis_index_groups=groups, tiled=True)  36.9 us
    all_to_all x1, blocking collectives, shards(): long = lax.all_to_all(smoothed, 'row', 0, 0, tiled=True)  22.8 us
    all_to_all x1, blocking collectives, shards(): tile = lax.all_to_all(back, 'row', 0, 0, tiled=True)  17.2 us
    all_to_all x1, blocking collectives, shards(): by_col = lax.all_to_all(lines, 'col', 0, 0, tiled=True)  14 us
    all_to_all x1, blocking collectives, shards(): by_row = lax.all_to_all(bands, 'row', 0, 0, tiled=True)  11.6 us
    ppermute x1, starting transfers between devices, shards(): lax.ppermute(own, 'col', [(block, block ^ 1) for block in range(COLS)])  4.95 us
  transfers between devices with their start and end apart: 1, of which 0 were waited for; matrix products, arithmetic and copies ran while one was open for 0% of the time, Pallas kernels for 1%

profile of v4, /device:TPU:1, one launch (start us, length us, event | category | flops | bytes accessed | tf_op | source)
XLA Modules:
  0.0 117.3 jit_solution(8454301099701296808)
XLA Ops:
  1.3 2.0 %source.1 = bf16[16,256,128]{2,1,0:T(8,128)(2,1)} custom-call(s32[1]{0:T(128)} %bitcast.place_ref, s32[1,1]{1,0:T(1,128)S(6)} %copy.13.region_ref, f32[128]{0:T(128)} %fill_in.1, f32[128,128]{1,0:T(8,128)} %height_ref.1, f32[128,128]{1,0:T(8,128)} %density_in.1), custom_call_target="tpu_custom_call" | custom-call | tf_op jit(solution)/shard_map/source/pallas_call | solution.py:331
  3.3 0.0 copy-start.2
  3.3 0.0 copy-start.3
  3.3 36.9 %all_to_all.25.after_ref.own_ref = bf16[16,256,128]{2,1,0:T(8,128)(2,1)S(1)} all-to-all(bf16[16,256,128]{2,1,0:T(8,128)(2,1)} %source.1), channel_id=1, replica_groups={{0,2,4,6,8,10,12,14,16,18,20,22,24,26,28,30},{1,3,5,7,9,11,13,15,17,19,..., dimensions={0} | all-to-all | bytes 2097152 | tf_op jit(solution)/shard_map/all_to_all | solution.py:346
  40.2 0.0 copy-start.4
  40.2 0.0 copy-start.5
  40.2 5.0 %collective-permute-start = (bf16[16,256,128]{2,1,0:T(8,128)(2,1)S(1)}, bf16[16,256,128]{2,1,0:T(8,128)(2,1)S(1)}, u32[]{:S(2)}, u32[]{:S(2)}) collective-permute-start(bf16[16,256,128]{2,1,0:T(8,128)(2,1)S(1)} %all_to_all.25.after_ref.own_ref), channel_id=1, source_target_pairs={{0,1},{1,0},{2,3},{3,2},{4,5},{5,4},{6,7},{7,6},{8,9},{9,8},{10,11... | collective-permute-start | bytes 3145736 | tf_op jit(solution)/shard_map/ppermute | solution.py:347
  45.8 0.0 copy-done.2
  45.8 0.0 copy-done.3
  45.8 0.0 copy-done.4
  45.8 0.0 copy-done.5
  45.8 0.0 copy-start
  45.8 0.0 copy-start.1
  45.9 1.6 %tables.1 = (bf16[128,384]{1,0:T(8,128)(2,1)S(1)}, bf16[128,384]{1,0:T(8,128)(2,1)S(1)}, bf16[128,384]{1,0:T(8,128)(2,1)S(1)}, bf16[128,384]{1,0:T(8,128)(2,1)S(...) custom-call(f32[8,33]{1,0:T(8,128)S(1)} %copy-done.2, ...), custom_call_target="tpu_custom_call" | custom-call | flops 4000000 | bytes 4000000 | tf_op jit(solution)/shard_map/tables/pallas_call | solution.py:349
  47.4 0.0 collective-permute-done.other_ref
  47.4 0.0 copy-done
  47.4 0.0 copy-done.1
  47.4 1.0 smooth.1
  48.4 22.8 %all_to_all.26.long_ref = bf16[16,80,128]{2,1,0:T(8,128)(2,1)S(1)} all-to-all(bf16[16,80,128]{2,1,0:T(8,128)(2,1)S(1)} %smooth.1), channel_id=1, replica_groups=mesh['row'=16,'col'=32] {'row'}, dimensions={0} | all-to-all | bytes 655360 | tf_op jit(solution)/shard_map/all_to_all | solution.py:386
  71.2 1.7 %pressure.1 = (bf16[16,80,128]{2,1,0:T(8,128)(2,1)S(1)}, f32[8,128]{1,0:T(8,128)S(1)}) custom-call(f32[16,8,128]{2,1,0:T(8,128)S(1)} %get-tuple-element.25.scales_ref, bf16[16,80,128]{2,1,0:T(8,128)(2,1)S(1)} %all_to_all.26.long_ref, f32[16,8,128]{2,1,0:T(8,128)S(1)} %get-tuple-element.34.last_ref, bf16[128,384]{1,0:T(8,128)(2,1)S(1)} %get-tuple-element.35.refs_0_, ...), custom_call_target="tpu_custom_call" | custom-call | tf_op jit(solution)/shard_map/pressure/pallas_call | solution.py:388
  73.0 17.2 %all_to_all.27.back_ref = bf16[16,80,128]{2,1,0:T(8,128)(2,1)S(1)} all-to-all(bf16[16,80,128]{2,1,0:T(8,128)(2,1)S(1)} %get-tuple-element.42), channel_id=1, replica_groups=mesh['row'=16,'col'=32] {'row'}, dimensions={0} | all-to-all | bytes 655360 | tf_op jit(solution)/shard_map/all_to_all | solution.py:396
  90.1 0.7 gradient.1
  90.9 14.0 %all_to_all.28.lines_ref = f32[32,1,128]{2,1,0:T(1,128)S(1)} all-to-all(f32[32,1,128]{2,1,0:T(1,128)S(1)} %gradient.1), channel_id=1, replica_groups=mesh['row'=16,'col'=32] {'col'}, dimensions={0} | all-to-all | bytes 32768 | tf_op jit(solution)/shard_map/all_to_all | solution.py:405
  104.9 0.1 band.1
  105.0 11.6 %all_to_all.29.bands_ref = f32[16,2,128]{2,1,0:T(2,128)S(1)} all-to-all(f32[16,2,128]{2,1,0:T(2,128)S(1)} %band.1), channel_id=1, replica_groups=mesh['row'=16,'col'=32] {'row'}, dimensions={0} | all-to-all | bytes 32768 | tf_op jit(solution)/shard_map/all_to_all | solution.py:414
  116.6 0.7 total.1
Async XLA Ops:
  3.3 42.5 %copy-start.2 = (f32[8,33]{1,0:T(8,128)S(1)}, f32[8,33]{1,0:T(8,128)}, u32[]{:S(2)}) copy-start(f32[8,33]{1,0:T(8,128)} %col_in.1) | copy-start | bytes 3172
  3.3 42.5 %copy-start.3 = (f32[8,33]{1,0:T(8,128)S(1)}, f32[8,33]{1,0:T(8,128)}, u32[]{:S(2)}) copy-start(f32[8,33]{1,0:T(8,128)} %row_in.1) | copy-start | bytes 3172
  40.2 5.6 %copy-start.4 = (f32[8]{0:T(128)S(1)}, f32[8]{0:T(128)}, u32[]{:S(2)}) copy-start(f32[8]{0:T(128)} %gains_in.1) | copy-start | bytes 100
  40.2 5.6 %copy-start.5 = (f32[8]{0:T(128)S(1)}, f32[8]{0:T(128)}, u32[]{:S(2)}) copy-start(f32[8]{0:T(128)} %rates_in.1) | copy-start | bytes 100
  40.2 7.2 %collective-permute-start = (bf16[16,256,128]{2,1,0:T(8,128)(2,1)S(1)}, bf16[16,256,128]{2,1,0:T(8,128)(2,1)S(1)}, u32[]{:S(2)}, u32[]{:S(2)}) collective-permute-start(bf16[16,256,128]{2,1,0:T(8,128)(2,1)S(1)} %all_to_all.25.after_ref.own_ref), channel_id=1, source_target_pairs={{0,1},{1,0},{2,3},{3,2},{4,5},{5,4},{6,7},{7,6},{8,9},{9,8},{10,11... | collective-permute-start | bytes 3145736 | tf_op jit(solution)/shard_map/ppermute | solution.py:347
  45.8 1.6 %copy-start = (f32[128,128]{1,0:T(8,128)S(1)}, f32[128,128]{1,0:T(8,128)}, u32[]{:S(2)}) copy-start(f32[128,128]{1,0:T(8,128)} %height_ref.1) | copy-start | bytes 196612
  45.8 1.6 %copy-start.1 = (f32[128,128]{1,0:T(8,128)S(1)}, f32[128,128]{1,0:T(8,128)}, u32[]{:S(2)}) copy-start(f32[128,128]{1,0:T(8,128)} %target_in.1) | copy-start | bytes 196612

commit v5 on v4

--- a/solution.py
+++ b/solution.py
@@ -17,6 +17,7 @@
 SUB = SIDE // ROWS
 MIXED = CHANNELS - 1
 F32 = jnp.float32
+BAND_ORDER = [2 * step + half for half in range(2) for step in range(ROWS // 2)]
 BF16 = jnp.bfloat16
 VMEM = pl.BlockSpec(memory_space=pltpu.VMEM)
 SMEM = pl.BlockSpec(memory_space=pltpu.SMEM)
@@ -50,6 +51,19 @@
     return (
         values[:, :SUB, :].reshape(SIDE, SIDE),
         values[:, SUB:, :].reshape(SIDE, SIDE),
+    )
+
+
+def along_rows(values):
+    return jnp.concatenate(
+        [values[SUB * p : SUB * p + SUB] for p in (b % 2 * (ROWS // 2) + b // 2 for b in range(ROWS))],
+        axis=0,
+    )
+
+
+def along_peers(values):
+    return jnp.concatenate(
+        [values[SUB * b : SUB * b + SUB] for b in BAND_ORDER], axis=0
     )
 
 
@@ -187,8 +201,9 @@
     tables, out_ref, gain_ref = refs[:MIXED], refs[MIXED], refs[MIXED + 1]
     smoothed = []
     for pair in range(CHANNELS // 2):
-        smoothed.extend(unpair_rows(long_ref[:, 16 * pair : 16 * pair + 16, :]))
-    high, low = unpair_rows(long_ref[:, 64:, :])
+        for values in unpair_rows(long_ref[:, 16 * pair : 16 * pair + 16, :]):
+            smoothed.append(along_rows(values))
+    high, low = map(along_rows, unpair_rows(long_ref[:, 64:, :]))
     low = low.reshape(ROWS, SUB, SIDE)
     row = lax.broadcasted_iota(jnp.int32, (ROWS, SUB, SIDE), 1)
     lane = lax.broadcasted_iota(jnp.int32, (ROWS, SUB, SIDE), 2)
@@ -244,9 +259,9 @@
         weighted.append(scaled(total, scales_ref[channel]))
     for pair in range(CHANNELS // 2):
         out_ref[:, 16 * pair : 16 * pair + 16, :] = pair_rows(
-            weighted[2 * pair], weighted[2 * pair + 1]
+            along_peers(weighted[2 * pair]), along_peers(weighted[2 * pair + 1])
         ).astype(BF16)
-    high, low = split(removed)
+    high, low = split(along_peers(removed))
     out_ref[:, 64:, :] = pair_rows(high.astype(F32), low.astype(F32)).astype(BF16)
     gain_ref[...] = jnp.concatenate(gain_rows, axis=0)
 
@@ -383,7 +398,7 @@
         compiler_params=PARAMS,
         name="smooth",
     )(place, class_of_block, own, other, height, target, col_last, *col_tables)
-    long = lax.all_to_all(smoothed, "row", 0, 0, tiled=True)
+    long = lax.all_to_all(smoothed, "row", 0, 0, axis_index_groups=[BAND_ORDER], tiled=True)
 
     back, gain_part = pl.pallas_call(
         pressure_kernel,
@@ -393,7 +408,7 @@
         compiler_params=PARAMS,
         name="pressure",
     )(scales, long, row_last, *row_tables)
-    tile = lax.all_to_all(back, "row", 0, 0, tiled=True)
+    tile = lax.all_to_all(back, "row", 0, 0, axis_index_groups=[BAND_ORDER], tiled=True)
     lines = pl.pallas_call(
         gradient_kernel,
         out_shape=shape(COLS, 1, SIDE),
@@ -411,7 +426,7 @@
         compiler_params=PARAMS,
         name="band",
     )(by_col)
-    by_row = lax.all_to_all(bands, "row", 0, 0, tiled=True)
+    by_row = lax.all_to_all(bands, "row", 0, 0, axis_index_groups=[BAND_ORDER], tiled=True)
     new_height, fill_grad, gain_grad = pl.pallas_call(
         total_kernel,
         out_shape=[shape(SIDE, SIDE), shape(SIDE), shape(CHANNELS)],

time: 118 us -> 117 us (level)
  no operation moved by 1% of the time
where the time goes in v5:
time: 117 us
  blocking collectives  102 us (87%)
  Pallas kernels  7.85 us (7%)
  starting transfers between devices  4.95 us (4%)
  between operations  2.06 us (2%)
    all_to_all x1, blocking collectives, shards(): lax.all_to_all(copies, 'col', 0, 0, axis_index_groups=groups, tiled=True)  36.9 us
    all_to_all x1, blocking collectives, shards(): lax.all_to_all(smoothed, 'row', 0, 0, axis_index_groups=[BAND_ORDER], til...  20.3 us
    all_to_all x1, blocking collectives, shards(): lax.all_to_all(back, 'row', 0, 0, axis_index_groups=[BAND_ORDER], tiled=T...  17 us
    all_to_all x1, blocking collectives, shards(): by_col = lax.all_to_all(lines, 'col', 0, 0, tiled=True)  14.5 us
    all_to_all x1, blocking collectives, shards(): lax.all_to_all(bands, 'row', 0, 0, axis_index_groups=[BAND_ORDER], tiled=...  13.4 us
    ppermute x1, starting transfers between devices, shards(): lax.ppermute(own, 'col', [(block, block ^ 1) for block in range(COLS)])  4.95 us
  transfers between devices with their start and end apart: 1, of which 0 were waited for; matrix products, arithmetic and copies ran while one was open for 0% of the time, Pallas kernels for 1%

profile of v5, /device:TPU:1, one launch (start us, length us, event | category | flops | bytes accessed | tf_op | source)
XLA Modules:
  0.0 117.0 jit_solution(9739122672782206471)
XLA Ops:
  1.3 2.0 %source.1 = bf16[16,256,128]{2,1,0:T(8,128)(2,1)} custom-call(s32[1]{0:T(128)} %bitcast.place_ref, s32[1,1]{1,0:T(1,128)S(6)} %copy.13.region_ref, f32[128]{0:T(128)} %fill_in.1, f32[128,128]{1,0:T(8,128)} %height_ref.1, f32[128,128]{1,0:T(8,128)} %density_in.1), custom_call_target="tpu_custom_call" | custom-call | tf_op jit(solution)/shard_map/source/pallas_call | solution.py:346
  3.3 0.0 copy-start.2
  3.3 0.0 copy-start.3
  3.3 36.9 %all_to_all.25.after_ref.own_ref = bf16[16,256,128]{2,1,0:T(8,128)(2,1)S(1)} all-to-all(bf16[16,256,128]{2,1,0:T(8,128)(2,1)} %source.1), channel_id=1, replica_groups={{0,2,4,6,8,10,12,14,16,18,20,22,24,26,28,30},{1,3,5,7,9,11,13,15,17,19,..., dimensions={0} | all-to-all | bytes 2097152 | tf_op jit(solution)/shard_map/all_to_all | solution.py:361
  40.2 0.0 copy-start.4
  40.2 0.0 copy-start.5
  40.2 5.0 %collective-permute-start = (bf16[16,256,128]{2,1,0:T(8,128)(2,1)S(1)}, bf16[16,256,128]{2,1,0:T(8,128)(2,1)S(1)}, u32[]{:S(2)}, u32[]{:S(2)}) collective-permute-start(bf16[16,256,128]{2,1,0:T(8,128)(2,1)S(1)} %all_to_all.25.after_ref.own_ref), channel_id=1, source_target_pairs={{0,1},{1,0},{2,3},{3,2},{4,5},{5,4},{6,7},{7,6},{8,9},{9,8},{10,11... | collective-permute-start | bytes 3145736 | tf_op jit(solution)/shard_map/ppermute | solution.py:362
  45.8 0.0 copy-done.2
  45.8 0.0 copy-done.3
  45.8 0.0 copy-done.4
  45.8 0.0 copy-done.5
  45.8 0.0 copy-start
  45.8 0.0 copy-start.1
  45.9 1.6 %tables.1 = (bf16[128,384]{1,0:T(8,128)(2,1)S(1)}, bf16[128,384]{1,0:T(8,128)(2,1)S(1)}, bf16[128,384]{1,0:T(8,128)(2,1)S(1)}, bf16[128,384]{1,0:T(8,128)(2,1)S(...) custom-call(f32[8,33]{1,0:T(8,128)S(1)} %copy-done.2, ...), custom_call_target="tpu_custom_call" | custom-call | flops 4000000 | bytes 4000000 | tf_op jit(solution)/shard_map/tables/pallas_call | solution.py:364
  47.4 0.0 collective-permute-done.other_ref
  47.4 0.0 copy-done
  47.4 0.0 copy-done.1
  47.4 1.0 smooth.1
  48.4 20.3 %all_to_all.26.long_ref = bf16[16,80,128]{2,1,0:T(8,128)(2,1)S(1)} all-to-all(bf16[16,80,128]{2,1,0:T(8,128)(2,1)S(1)} %smooth.1), channel_id=1, replica_groups={{0,64,128,192,256,320,384,448,32,96,160,224,288,352,416,480},{1,65,129,..., dimensions={0} | all-to-all | bytes 655360 | tf_op jit(solution)/shard_map/all_to_all | solution.py:401
  68.7 1.7 %pressure.1 = (bf16[16,80,128]{2,1,0:T(8,128)(2,1)S(1)}, f32[8,128]{1,0:T(8,128)S(1)}) custom-call(f32[16,8,128]{2,1,0:T(8,128)S(1)} %get-tuple-element.25.scales_ref, bf16[16,80,128]{2,1,0:T(8,128)(2,1)S(1)} %all_to_all.26.long_ref, f32[16,8,128]{2,1,0:T(8,128)S(1)} %get-tuple-element.34.last_ref, bf16[128,384]{1,0:T(8,128)(2,1)S(1)} %get-tuple-element.35.refs_0_, ...), custom_call_target="tpu_custom_call" | custom-call | tf_op jit(solution)/shard_map/pressure/pallas_call | solution.py:403
  70.5 17.0 %all_to_all.27.back_ref = bf16[16,80,128]{2,1,0:T(8,128)(2,1)S(1)} all-to-all(bf16[16,80,128]{2,1,0:T(8,128)(2,1)S(1)} %get-tuple-element.42), channel_id=1, replica_groups={{0,64,128,192,256,320,384,448,32,96,160,224,288,352,416,480},{1,65,129,..., dimensions={0} | all-to-all | bytes 655360 | tf_op jit(solution)/shard_map/all_to_all | solution.py:411
  87.5 0.7 gradient.1
  88.2 14.5 %all_to_all.28.lines_ref = f32[32,1,128]{2,1,0:T(1,128)S(1)} all-to-all(f32[32,1,128]{2,1,0:T(1,128)S(1)} %gradient.1), channel_id=1, replica_groups=mesh['row'=16,'col'=32] {'col'}, dimensions={0} | all-to-all | bytes 32768 | tf_op jit(solution)/shard_map/all_to_all | solution.py:420
  102.7 0.1 band.1
  102.9 13.4 %all_to_all.29.bands_ref = f32[16,2,128]{2,1,0:T(2,128)S(1)} all-to-all(f32[16,2,128]{2,1,0:T(2,128)S(1)} %band.1), channel_id=1, replica_groups={{0,64,128,192,256,320,384,448,32,96,160,224,288,352,416,480},{1,65,129,..., dimensions={0} | all-to-all | bytes 32768 | tf_op jit(solution)/shard_map/all_to_all | solution.py:429
  116.2 0.7 total.1
Async XLA Ops:
  3.3 42.5 %copy-start.2 = (f32[8,33]{1,0:T(8,128)S(1)}, f32[8,33]{1,0:T(8,128)}, u32[]{:S(2)}) copy-start(f32[8,33]{1,0:T(8,128)} %col_in.1) | copy-start | bytes 3172
  3.3 42.5 %copy-start.3 = (f32[8,33]{1,0:T(8,128)S(1)}, f32[8,33]{1,0:T(8,128)}, u32[]{:S(2)}) copy-start(f32[8,33]{1,0:T(8,128)} %row_in.1) | copy-start | bytes 3172
  40.2 5.6 %copy-start.4 = (f32[8]{0:T(128)S(1)}, f32[8]{0:T(128)}, u32[]{:S(2)}) copy-start(f32[8]{0:T(128)} %gains_in.1) | copy-start | bytes 100
  40.2 5.6 %copy-start.5 = (f32[8]{0:T(128)S(1)}, f32[8]{0:T(128)}, u32[]{:S(2)}) copy-start(f32[8]{0:T(128)} %rates_in.1) | copy-start | bytes 100
  40.2 7.2 %collective-permute-start = (bf16[16,256,128]{2,1,0:T(8,128)(2,1)S(1)}, bf16[16,256,128]{2,1,0:T(8,128)(2,1)S(1)}, u32[]{:S(2)}, u32[]{:S(2)}) collective-permute-start(bf16[16,256,128]{2,1,0:T(8,128)(2,1)S(1)} %all_to_all.25.after_ref.own_ref), channel_id=1, source_target_pairs={{0,1},{1,0},{2,3},{3,2},{4,5},{5,4},{6,7},{7,6},{8,9},{9,8},{10,11... | collective-permute-start | bytes 3145736 | tf_op jit(solution)/shard_map/ppermute | solution.py:362
  45.8 1.6 %copy-start = (f32[128,128]{1,0:T(8,128)S(1)}, f32[128,128]{1,0:T(8,128)}, u32[]{:S(2)}) copy-start(f32[128,128]{1,0:T(8,128)} %height_ref.1) | copy-start | bytes 196612
  45.8 1.6 %copy-start.1 = (f32[128,128]{1,0:T(8,128)S(1)}, f32[128,128]{1,0:T(8,128)}, u32[]{:S(2)}) copy-start(f32[128,128]{1,0:T(8,128)} %target_in.1) | copy-start | bytes 196612

commit v6 on v5

--- a/solution.py
+++ b/solution.py
@@ -310,7 +310,8 @@
     row = lax.broadcasted_iota(jnp.int32, (COLS, SIDE), 0)
     lane = lax.broadcasted_iota(jnp.int32, (COLS, SIDE), 1)
     band = jnp.sum(lines, axis=0, keepdims=True)
-    held = jnp.sum(jnp.where(lane == row, band, 0.0), axis=1, keepdims=True)
+    sender = 2 * (row % PEERS) + row // PEERS
+    held = jnp.sum(jnp.where(lane == sender, band, 0.0), axis=1, keepdims=True)
     region = jnp.sum(jnp.where(lane == 2 * COLS, lines, 0.0), axis=1, keepdims=True)
     fill = jnp.where(region == lane.astype(F32), held, 0.0)
     both = jnp.concatenate([jnp.sum(fill, axis=0, keepdims=True), band], axis=0)
@@ -417,7 +418,9 @@
         compiler_params=PARAMS,
         name="gradient",
     )(place, region_of_block, tile, own, other, gain_part, col_last, *col_tables)
-    by_col = lax.all_to_all(lines, "col", 0, 0, tiled=True)
+    by_col = lax.all_to_all(
+        lines, "col", 0, 0, axis_index_groups=[groups[0] + groups[1]], tiled=True
+    )
     bands = pl.pallas_call(
         band_kernel,
         out_shape=shape(ROWS, 2, SIDE),

time: 117 us -> 117 us (level)
  no operation moved by 1% of the time
where the time goes in v6:
time: 117 us
  blocking collectives  102 us (87%)
  Pallas kernels  7.85 us (7%)
  starting transfers between devices  4.95 us (4%)
  between operations  2.06 us (2%)
    all_to_all x1, blocking collectives, shards(): lax.all_to_all(copies, 'col', 0, 0, axis_index_groups=groups, tiled=True)  36.9 us
    all_to_all x1, blocking collectives, shards(): lax.all_to_all(smoothed, 'row', 0, 0, axis_index_groups=[BAND_ORDER], til...  20.3 us
    all_to_all x1, blocking collectives, shards(): lax.all_to_all(back, 'row', 0, 0, axis_index_groups=[BAND_ORDER], tiled=T...  17 us
    all_to_all x1, blocking collectives, shards(): lax.all_to_all(lines, 'col', 0, 0, axis_index_groups=[groups[0] + groups[...  14.5 us
    all_to_all x1, blocking collectives, shards(): lax.all_to_all(bands, 'row', 0, 0, axis_index_groups=[BAND_ORDER], tiled=...  13.4 us
    ppermute x1, starting transfers between devices, shards(): lax.ppermute(own, 'col', [(block, block ^ 1) for block in range(COLS)])  4.95 us
  transfers between devices with their start and end apart: 1, of which 0 were waited for; matrix products, arithmetic and copies ran while one was open for 0% of the time, Pallas kernels for 1%

profile of v6, /device:TPU:1, one launch (start us, length us, event | category | flops | bytes accessed | tf_op | source)
XLA Modules:
  0.0 116.9 jit_solution(7755762064332165087)
XLA Ops:
  1.3 2.0 %source.1 = bf16[16,256,128]{2,1,0:T(8,128)(2,1)} custom-call(s32[1]{0:T(128)} %bitcast.place_ref, s32[1,1]{1,0:T(1,128)S(6)} %copy.13.region_ref, f32[128]{0:T(128)} %fill_in.1, f32[128,128]{1,0:T(8,128)} %height_ref.1, f32[128,128]{1,0:T(8,128)} %density_in.1), custom_call_target="tpu_custom_call" | custom-call | tf_op jit(solution)/shard_map/source/pallas_call | solution.py:347
  3.3 0.0 copy-start.2
  3.3 0.0 copy-start.3
  3.3 36.9 %all_to_all.25.after_ref.own_ref = bf16[16,256,128]{2,1,0:T(8,128)(2,1)S(1)} all-to-all(bf16[16,256,128]{2,1,0:T(8,128)(2,1)} %source.1), channel_id=1, replica_groups={{0,2,4,6,8,10,12,14,16,18,20,22,24,26,28,30},{1,3,5,7,9,11,13,15,17,19,..., dimensions={0} | all-to-all | bytes 2097152 | tf_op jit(solution)/shard_map/all_to_all | solution.py:362
  40.2 0.0 copy-start.4
  40.2 0.0 copy-start.5
  40.2 5.0 %collective-permute-start = (bf16[16,256,128]{2,1,0:T(8,128)(2,1)S(1)}, bf16[16,256,128]{2,1,0:T(8,128)(2,1)S(1)}, u32[]{:S(2)}, u32[]{:S(2)}) collective-permute-start(bf16[16,256,128]{2,1,0:T(8,128)(2,1)S(1)} %all_to_all.25.after_ref.own_ref), channel_id=1, source_target_pairs={{0,1},{1,0},{2,3},{3,2},{4,5},{5,4},{6,7},{7,6},{8,9},{9,8},{10,11... | collective-permute-start | bytes 3145736 | tf_op jit(solution)/shard_map/ppermute | solution.py:363
  45.8 0.0 copy-done.2
  45.8 0.0 copy-done.3
  45.8 0.0 copy-done.4
  45.8 0.0 copy-done.5
  45.8 0.0 copy-start
  45.8 0.0 copy-start.1
  45.9 1.6 %tables.1 = (bf16[128,384]{1,0:T(8,128)(2,1)S(1)}, bf16[128,384]{1,0:T(8,128)(2,1)S(1)}, bf16[128,384]{1,0:T(8,128)(2,1)S(1)}, bf16[128,384]{1,0:T(8,128)(2,1)S(...) custom-call(f32[8,33]{1,0:T(8,128)S(1)} %copy-done.2, ...), custom_call_target="tpu_custom_call" | custom-call | flops 4000000 | bytes 4000000 | tf_op jit(solution)/shard_map/tables/pallas_call | solution.py:365
  47.4 0.0 collective-permute-done.other_ref
  47.4 0.0 copy-done
  47.4 0.0 copy-done.1
  47.4 1.0 smooth.1
  48.4 20.3 %all_to_all.26.long_ref = bf16[16,80,128]{2,1,0:T(8,128)(2,1)S(1)} all-to-all(bf16[16,80,128]{2,1,0:T(8,128)(2,1)S(1)} %smooth.1), channel_id=1, replica_groups={{0,64,128,192,256,320,384,448,32,96,160,224,288,352,416,480},{1,65,129,..., dimensions={0} | all-to-all | bytes 655360 | tf_op jit(solution)/shard_map/all_to_all | solution.py:402
  68.7 1.7 %pressure.1 = (bf16[16,80,128]{2,1,0:T(8,128)(2,1)S(1)}, f32[8,128]{1,0:T(8,128)S(1)}) custom-call(f32[16,8,128]{2,1,0:T(8,128)S(1)} %get-tuple-element.25.scales_ref, bf16[16,80,128]{2,1,0:T(8,128)(2,1)S(1)} %all_to_all.26.long_ref, f32[16,8,128]{2,1,0:T(8,128)S(1)} %get-tuple-element.34.last_ref, bf16[128,384]{1,0:T(8,128)(2,1)S(1)} %get-tuple-element.35.refs_0_, ...), custom_call_target="tpu_custom_call" | custom-call | tf_op jit(solution)/shard_map/pressure/pallas_call | solution.py:404
  70.5 17.0 %all_to_all.27.back_ref = bf16[16,80,128]{2,1,0:T(8,128)(2,1)S(1)} all-to-all(bf16[16,80,128]{2,1,0:T(8,128)(2,1)S(1)} %get-tuple-element.42), channel_id=1, replica_groups={{0,64,128,192,256,320,384,448,32,96,160,224,288,352,416,480},{1,65,129,..., dimensions={0} | all-to-all | bytes 655360 | tf_op jit(solution)/shard_map/all_to_all | solution.py:412
  87.5 0.7 gradient.1
  88.2 14.5 %all_to_all.28.lines_ref = f32[32,1,128]{2,1,0:T(1,128)S(1)} all-to-all(f32[32,1,128]{2,1,0:T(1,128)S(1)} %gradient.1), channel_id=1, replica_groups={{0,2,4,6,8,10,12,14,16,18,20,22,24,26,28,30,1,3,5,7,9,11,13,15,17,19,21..., dimensions={0} | all-to-all | bytes 32768 | tf_op jit(solution)/shard_map/all_to_all | solution.py:421
  102.7 0.1 band.1
  102.8 13.4 %all_to_all.29.bands_ref = f32[16,2,128]{2,1,0:T(2,128)S(1)} all-to-all(f32[16,2,128]{2,1,0:T(2,128)S(1)} %band.1), channel_id=1, replica_groups={{0,64,128,192,256,320,384,448,32,96,160,224,288,352,416,480},{1,65,129,..., dimensions={0} | all-to-all | bytes 32768 | tf_op jit(solution)/shard_map/all_to_all | solution.py:432
  116.2 0.7 total.1
Async XLA Ops:
  3.3 42.5 %copy-start.2 = (f32[8,33]{1,0:T(8,128)S(1)}, f32[8,33]{1,0:T(8,128)}, u32[]{:S(2)}) copy-start(f32[8,33]{1,0:T(8,128)} %col_in.1) | copy-start | bytes 3172
  3.3 42.5 %copy-start.3 = (f32[8,33]{1,0:T(8,128)S(1)}, f32[8,33]{1,0:T(8,128)}, u32[]{:S(2)}) copy-start(f32[8,33]{1,0:T(8,128)} %row_in.1) | copy-start | bytes 3172
  40.2 5.6 %copy-start.4 = (f32[8]{0:T(128)S(1)}, f32[8]{0:T(128)}, u32[]{:S(2)}) copy-start(f32[8]{0:T(128)} %gains_in.1) | copy-start | bytes 100
  40.2 5.6 %copy-start.5 = (f32[8]{0:T(128)S(1)}, f32[8]{0:T(128)}, u32[]{:S(2)}) copy-start(f32[8]{0:T(128)} %rates_in.1) | copy-start | bytes 100
  40.2 7.2 %collective-permute-start = (bf16[16,256,128]{2,1,0:T(8,128)(2,1)S(1)}, bf16[16,256,128]{2,1,0:T(8,128)(2,1)S(1)}, u32[]{:S(2)}, u32[]{:S(2)}) collective-permute-start(bf16[16,256,128]{2,1,0:T(8,128)(2,1)S(1)} %all_to_all.25.after_ref.own_ref), channel_id=1, source_target_pairs={{0,1},{1,0},{2,3},{3,2},{4,5},{5,4},{6,7},{7,6},{8,9},{9,8},{10,11... | collective-permute-start | bytes 3145736 | tf_op jit(solution)/shard_map/ppermute | solution.py:363
  45.8 1.6 %copy-start = (f32[128,128]{1,0:T(8,128)S(1)}, f32[128,128]{1,0:T(8,128)}, u32[]{:S(2)}) copy-start(f32[128,128]{1,0:T(8,128)} %height_ref.1) | copy-start | bytes 196612
  45.8 1.6 %copy-start.1 = (f32[128,128]{1,0:T(8,128)S(1)}, f32[128,128]{1,0:T(8,128)}, u32[]{:S(2)}) copy-start(f32[128,128]{1,0:T(8,128)} %target_in.1) | copy-start | bytes 196612
